TPU v7x, 128 devices: a whole 4x4x4 slice. The times are simulated.
128 devices in a mesh: attn: 8 (over y, core), exp: 16 (over x, z).
Axes of the slice: x: 4, y: 4, z: 4, core: 2. Of those that a mesh axis runs over, the one named last changes fastest.
Arguments:
- moe_in: bfloat16 [768, 7168], P(('attn', 'exp')), may hold values from -6 to 6
- routes: int32 [768, 2], P(('attn', 'exp')), may hold values from 0 to 15, all different within a row; in each aligned block of 6 rows (0 to 5, 6 to 11, ...) at most 2 rows name the same one
- gates: float32 [768, 2], P(('attn', 'exp')), may hold values from 0.2 to 1
- gate_w: bfloat16 [16, 7168, 2048], P('exp', None, 'attn'), may hold values from -0.0625 to 0.0625
- up_w: bfloat16 [16, 7168, 2048], P('exp', None, 'attn'), may hold values from -0.0625 to 0.0625
- down_w: bfloat16 [16, 2048, 7168], P('exp', 'attn'), may hold values from -0.125 to 0.125
- queries: bfloat16 [512, 128, 576], P(('attn', 'exp')), may hold values from -55 to 55
- latent_cache: bfloat16 [512, 2048, 576], P(('attn', 'exp')), may hold values from -4 to 4
- lengths: int32 [512], P(('attn', 'exp')), may hold values from 2 to 2048, as said below
Outputs:
- moe_out: bfloat16 [768, 7168], P(('attn', 'exp'))
- attended: bfloat16 [512, 128, 512], P(('attn', 'exp'))
Inputs may be any that keep to these rules, and one draw needn't show every extreme that they name: `routes`: each row names 2 different experts; among the rows of one device no expert is named more than 2 times, and in every draw some expert is named exactly 2 times by the rows of some device. Row r attends to cache positions below lengths[r]; some row has all 2048.
All inputs are finite; a program needn't handle non-finite values.
Results may differ from a plain program's by a relative error of at most 0.015.
Values may be sent and summed in bfloat16 or wider, within the bound.
No kernel may reach another device: no remote copies, remote signals or barrier semaphores. Data moves between devices by JAX's collectives and lax.ppermute only.
A program may use at most 128 MiB of HBM per device.

v0:
```python
import jax
import jax.numpy as jnp
from jax import lax
from jax.sharding import PartitionSpec as P

KV = 512


score_scale = 192.0 ** (-0.5)


def attend(queries, latent_cache, lengths):
    scores = (
        jnp.einsum("rhq,rtq->rht", queries, latent_cache, preferred_element_type=jnp.float32)
        * score_scale
    )
    position = jnp.arange(latent_cache.shape[1], dtype=jnp.int32)
    visible = position[None, None, :] < lengths[:, None, None]
    scores = jnp.where(visible, scores, -1e30)
    row_max = jnp.max(scores, axis=2, keepdims=True)
    exp_scores = jnp.where(visible, jnp.exp(scores - row_max), 0.0)
    probs = (exp_scores / jnp.sum(exp_scores, axis=2, keepdims=True)).astype(jnp.bfloat16)
    values = latent_cache[:, :, :KV]
    return jnp.einsum("rht,rtv->rhv", probs, values, preferred_element_type=jnp.float32).astype(
        jnp.bfloat16
    )


def body(moe_in, routes, gates, gate_w, up_w, down_w, queries, latent_cache, lengths):
    attended = attend(queries, latent_cache, lengths)
    rows_here, top_count = routes.shape
    local_count = gate_w.shape[0]
    experts = local_count * lax.axis_size("exp")
    attn_count = lax.axis_size("attn")
    model_width = moe_in.shape[1]
    slice_width = gate_w.shape[2]
    capacity = max(2, 2 * rows_here * top_count // experts)
    flat_routes = routes.reshape(-1)
    one_hot = (flat_routes[:, None] == jnp.arange(experts, dtype=jnp.int32)[None, :]).astype(
        jnp.int32
    )
    earlier = jnp.cumsum(one_hot, axis=0) - one_hot
    slot_ids = jnp.sum(earlier * one_hot, axis=1)
    targets = (slot_ids * experts + flat_routes).reshape(rows_here, top_count)
    selector = jnp.sum(
        (
            targets[None, :, :] == jnp.arange(capacity * experts, dtype=jnp.int32)[:, None, None]
        ).astype(jnp.float32),
        axis=2,
    ).astype(jnp.bfloat16)
    outgoing = jnp.dot(selector, moe_in, preferred_element_type=jnp.float32).astype(jnp.bfloat16)
    outgoing = outgoing.reshape(capacity, experts, model_width)
    outgoing_all = jnp.broadcast_to(outgoing[:, None], (capacity, attn_count, experts, model_width))
    outgoing_all = outgoing_all.reshape(capacity, attn_count * experts, model_width)
    block_rows = lax.all_to_all(
        outgoing_all, ("attn", "exp"), split_axis=1, concat_axis=1, tiled=True
    )
    slots = block_rows.shape[0]
    sources = block_rows.shape[1] // local_count
    shaped = block_rows.reshape(slots, sources, local_count, model_width)
    gate_act = jnp.einsum("csed,edf->csef", shaped, gate_w, preferred_element_type=jnp.float32)
    up_act = jnp.einsum("csed,edf->csef", shaped, up_w, preferred_element_type=jnp.float32)
    hidden = (jax.nn.silu(gate_act) * up_act).astype(jnp.bfloat16)
    hidden = hidden.reshape(slots, sources * local_count, slice_width)
    sources = hidden.shape[1] // local_count
    shaped = hidden.reshape(capacity, sources, local_count, slice_width)
    partial_value = jnp.einsum("csef,efd->csed", shaped, down_w, preferred_element_type=jnp.float32)
    partial_value = partial_value.reshape(capacity, sources * local_count, model_width).astype(
        jnp.bfloat16
    )
    returned = lax.all_to_all(
        partial_value, ("attn", "exp"), split_axis=1, concat_axis=1, tiled=True
    )
    returned = returned.reshape(capacity, attn_count, experts, model_width)
    results = jnp.sum(returned.astype(jnp.float32), axis=1).astype(jnp.bfloat16)
    picked = results.reshape(capacity * experts, model_width)[targets]
    moe_out = jnp.sum(picked.astype(jnp.float32) * gates[:, :, None], axis=1).astype(jnp.bfloat16)
    return (moe_out, attended)


def solution(mesh):
    placed = (
        P(("attn", "exp"), None),
        P(("attn", "exp"), None),
        P(("attn", "exp"), None),
        P("exp", None, "attn"),
        P("exp", None, "attn"),
        P("exp", "attn", None),
        P(("attn", "exp"), None, None),
        P(("attn", "exp"), None, None),
        P(("attn", "exp")),
    )
    return jax.shard_map(
        body,
        mesh=mesh,
        in_specs=placed,
        out_specs=(P(("attn", "exp"), None), P(("attn", "exp"), None, None)),
        check_vma=False,
    )
```

profile of v0, /device:TPU:0, one launch (start us, length us, event | category | flops | bytes accessed | tf_op | source)
XLA Modules:
  0.0 133.5 jit_solution(1100564017593509386)
XLA Ops:
  0.6 0.8 copy.36
  1.5 0.1 eq.28
  1.7 0.2 select_reduce_fusion
  1.9 0.1 fusion.44
  2.0 1.2 convolution_convert_fusion.1
  3.3 0.5 copy.38
  3.8 1.9 %broadcast_in_dim.36 = bf16[2,8,16,7168]{3,0,2,1:T(2,128)(2,1)S(1)} broadcast(bf16[2,16,7168]{2,0,1:T(2,128)(2,1)S(1)} %copy.38), dimensions={0,2,3} | broadcast | bytes 4128768 | tf_op jit(solution)/shard_map/broadcast_in_dim | solution.py:53
  5.7 57.3 %all_to_all.10 = bf16[2,128,7168]{2,0,1:T(2,128)(2,1)S(1)} all-to-all(bf16[2,128,7168]{2,0,1:T(2,128)(2,1)S(1)} %bitcast.51), channel_id=1, replica_groups=mesh['attn'=8,'exp'=16] {'attn','exp'}, dimensions={1} | all-to-all | bytes 7340032 | tf_op jit(solution)/shard_map/all_to_all | solution.py:55
  62.9 1.1 fusion.18
  64.1 0.9 copy-done.5
  65.0 1.1 fusion.38
  66.1 0.9 copy-done.1
  67.0 1.1 convolution_convert_fusion
  68.2 5.7 %copy.41 = bf16[2,128,7168]{2,0,1:T(2,128)(2,1)} copy(bf16[2,128,7168]{2,1,0:T(8,128)(2,1)S(1)} %convolution_convert_fusion) | data formatting | bytes 7340032 | tf_op jit(solution)/shard_map/convert_element_type | solution.py:68
  73.9 6.1 %all-to-all-start.1 = ((bf16[2,128,7168]{2,0,1:T(2,128)(2,1)}), bf16[2,128,7168]{2,0,1:T(2,128)(2,1)}, u32[]{:S(2)}, u32[]{:S(2)}) async-start(bf16[2,128,7168]{2,0,1:T(2,128)(2,1)} %copy.41), calls=%async_computation.1 | async-start | bytes 7340032 | tf_op jit(solution)/shard_map/all_to_all | solution.py:71
  80.0 0.1 copy.43
  80.1 0.1 iota_compare_fusion
  80.2 8.5 %fusion.48 = (f32[4,128]{1,0:T(4,128)S(1)}, f32[4,128,2048]{2,1,0:T(8,128)}) fusion(pred[4,2048]{1,0:T(4,128)(4,1)S(1)} %iota_compare_fusion, bf16[4,128,576]{1,2,0:T(8,128)(2,1)S(1)} %copy-done, bf16[4,2048,576]{1,2,0:T(8,128)(2,1)} %param.16), kind=kOutput, calls=%fused_computation.40 | convolution fusion | flops 1213204480 | bytes 14231552 | tf_op jit(solution)/shard_map/sub | solution.py:21
  88.7 8.4 %fusion.15 = bf16[4,128,512]{2,1,0:T(8,128)(2,1)} fusion(bf16[4,2048,576]{1,2,0:T(8,128)(2,1)} %param.16, f32[4,128,2048]{2,1,0:T(8,128)} %get-tuple-element.5, f32[4,128]{1,0:T(4,128)S(1)} %get-tuple-element.4), kind=kOutput, calls=%fused_computation.21 | convolution fusion | flops 1076101120 | bytes 13109248 | tf_op jit(solution)/shard_map/rht,rtv->rhv/dot_general | solution.py:24
  97.1 28.6 %all-to-all-done.1 = bf16[2,128,7168]{2,0,1:T(2,128)(2,1)} async-done(((bf16[2,128,7168]{2,0,1:T(2,128)(2,1)}), bf16[2,128,7168]{2,0,1:T(2,128)(2,1)}, u32[]{:S(2)}, u32[]{:S(2)}) %all-to-all-start.1) | async-done | bytes 3670048 | tf_op jit(solution)/shard_map/all_to_all | solution.py:71
  125.7 5.7 %reduce_sum.50 = bf16[2,16,7168]{2,0,1:T(2,128)(2,1)S(1)} reduce(bf16[2,8,16,7168]{3,0,2,1:T(2,128)(2,1)} %bitcast.17, bf16[]{:T(256)} %constant.8.clone.1), dimensions={1}, to_apply=%region_3.4 | reduce | flops 1605632 | bytes 4128770 | tf_op jit(solution)/shard_map/reduce_sum | solution.py:75
  131.5 0.7 gather_fusion
  132.1 0.2 reshape.88
  132.4 1.1 multiply_reduce_fusion
  (18 shorter events, 0.4 us)
Async XLA Ops:
  0.6 79.6 %copy-start = (bf16[4,128,576]{1,2,0:T(8,128)(2,1)S(1)}, bf16[4,128,576]{1,2,0:T(8,128)(2,1)}, u32[]{:S(2)}) copy-start(bf16[4,128,576]{1,2,0:T(8,128)(2,1)} %param.15) | copy-start | bytes 1769476
  5.7 57.3 %copy-start.4 = (bf16[1,7168,256]{2,1,0:T(8,128)(2,1)S(1)}, bf16[1,7168,256]{2,1,0:T(8,128)(2,1)}, u32[]{:S(2)}) copy-start(bf16[1,7168,256]{2,1,0:T(8,128)(2,1)} %param.12) | copy-start | bytes 11010052
  62.9 2.0 %copy-start.5 = (bf16[1,7168,256]{2,1,0:T(8,128)(2,1)S(1)}, bf16[1,7168,256]{2,1,0:T(8,128)(2,1)}, u32[]{:S(2)}) copy-start(bf16[1,7168,256]{2,1,0:T(8,128)(2,1)} %param.13) | copy-start | bytes 11010052
  65.0 2.0 %copy-start.1 = (bf16[1,256,7168]{2,1,0:T(8,128)(2,1)S(1)}, bf16[1,256,7168]{2,1,0:T(8,128)(2,1)}, u32[]{:S(2)}) copy-start(bf16[1,256,7168]{2,1,0:T(8,128)(2,1)} %param.14) | copy-start | bytes 11010052
  73.9 6.2 %copy-start.2 = (f32[6,2]{0,1:T(2,128)S(1)}, f32[6,2]{0,1:T(2,128)}, u32[]{:S(2)}) copy-start(f32[6,2]{0,1:T(2,128)} %param.11) | copy-start | bytes 148
  73.9 6.2 %copy-start.3 = (s32[4]{0:T(128)S(1)}, s32[4]{0:T(128)}, u32[]{:S(2)}) copy-start(s32[4]{0:T(128)} %param.17) | copy-start | bytes 52
  73.9 51.8 %all-to-all-start.1 = ((bf16[2,128,7168]{2,0,1:T(2,128)(2,1)}), bf16[2,128,7168]{2,0,1:T(2,128)(2,1)}, u32[]{:S(2)}, u32[]{:S(2)}) async-start(bf16[2,128,7168]{2,0,1:T(2,128)(2,1)} %copy.41), calls=%async_computation.1 | async-start | bytes 7340032 | tf_op jit(solution)/shard_map/all_to_all | solution.py:71
where the time goes:
time: 135 us; the launch traced here: 133 us
  blocking collectives  57.3 us (42%)
  waiting for transfers between devices  28.6 us (21%)
  matrix products  21.5 us (16%)
  local copies, waits for them, and re-layouts  12 us (9%)
  other arithmetic  7.3 us (5%)
  starting transfers between devices  6.06 us (4%)
    all_to_all x1, blocking collectives, body(): lax.all_to_all(outgoing_all, ('attn', 'exp'), split_axis=1, concat_axis=1...  57.3 us
    all_to_all x1, waiting for transfers between devices, body(): lax.all_to_all(partial_value, ('attn', 'exp'), split_axis=1, concat_axis=...  28.6 us
    sub x1, matrix products, attend(): exp_scores = jnp.where(visible, jnp.exp(scores - row_max), 0.0)  8.51 us
    dot_general x1, matrix products, attend(): jnp.einsum('rht,rtv->rhv', probs, values, preferred_element_type=jnp.floa...  8.36 us
    all_to_all x1, starting transfers between devices, body(): lax.all_to_all(partial_value, ('attn', 'exp'), split_axis=1, concat_axis=...  6.06 us
    convert_element_type x1, local copies, waits for them, and re-layouts, body(): partial_value.reshape(capacity, sources * local_count, model_width)  5.7 us
    reduce_sum x1, other arithmetic, body(): results = jnp.sum(returned.astype(jnp.float32), axis=1).astype(jnp.bfloat16)  5.66 us
    unnamed x14, local copies, waits for them, and re-layouts  2.77 us
  transfers between devices with their start and end apart: 1, of which 1 were waited for; matrix products, arithmetic and copies ran while one was open for 13% of the time, Pallas kernels for 0%

commit v1 on v0

v1 whole, which is shorter than its diff:
```python
import jax
import jax.numpy as jnp
from jax import lax
from jax.sharding import Mesh, PartitionSpec as P

KV = 512


score_scale = 192.0 ** (-0.5)


def attend(queries, latent_cache, lengths):
    scores = (
        jnp.einsum("rhq,rtq->rht", queries, latent_cache, preferred_element_type=jnp.float32)
        * score_scale
    )
    position = jnp.arange(latent_cache.shape[1], dtype=jnp.int32)
    visible = position[None, None, :] < lengths[:, None, None]
    scores = jnp.where(visible, scores, -1e30)
    row_max = jnp.max(scores, axis=2, keepdims=True)
    exp_scores = jnp.where(visible, jnp.exp(scores - row_max), 0.0)
    probs = (exp_scores / jnp.sum(exp_scores, axis=2, keepdims=True)).astype(jnp.bfloat16)
    values = latent_cache[:, :, :KV]
    return jnp.einsum("rht,rtv->rhv", probs, values, preferred_element_type=jnp.float32).astype(
        jnp.bfloat16
    )


def expert_slice(rows, gate_w, up_w, down_w):
    shape = rows.shape
    rows = rows.reshape(-1, shape[-1])
    gate_act = jnp.dot(rows, gate_w, preferred_element_type=jnp.float32)
    up_act = jnp.dot(rows, up_w, preferred_element_type=jnp.float32)
    hidden = (jax.nn.silu(gate_act) * up_act).astype(jnp.bfloat16)
    out = jnp.dot(hidden, down_w, preferred_element_type=jnp.float32)
    return out.astype(jnp.bfloat16).reshape(shape)


def body(moe_in, routes, gates, gate_w, up_w, down_w, queries, latent_cache, lengths):
    rows_here, top_count = routes.shape
    experts = lax.axis_size("x") * lax.axis_size("z")
    columns = lax.axis_size("y")
    chips = ("y", "x", "z")
    width = moe_in.shape[1]
    capacity = 2
    flat_routes = routes.reshape(-1)
    one_hot = (flat_routes[:, None] == jnp.arange(experts, dtype=jnp.int32)[None, :]).astype(
        jnp.int32
    )
    earlier = jnp.cumsum(one_hot, axis=0) - one_hot
    slot_ids = jnp.sum(earlier * one_hot, axis=1)
    targets = (flat_routes * capacity + slot_ids).reshape(rows_here, top_count)
    places = jnp.arange(capacity * experts, dtype=jnp.int32)
    named = targets[:, :, None] == places[None, None, :]
    selector = jnp.sum(named.astype(jnp.float32), axis=1).astype(jnp.bfloat16)
    outgoing = jnp.dot(selector.T, moe_in, preferred_element_type=jnp.float32).astype(jnp.bfloat16)
    outgoing = outgoing.reshape(1, experts, capacity, width)
    outgoing = jnp.broadcast_to(outgoing, (columns, experts, capacity, width))
    outgoing = outgoing.reshape(columns * experts, capacity, width)
    mine = lax.all_to_all(outgoing, chips, split_axis=0, concat_axis=0, tiled=True)
    swap = [(0, 1), (1, 0)]
    theirs = lax.ppermute(mine, "core", swap)
    weights = (gate_w[0], up_w[0], down_w[0])
    part_mine = expert_slice(mine, *weights)
    part_theirs = expert_slice(theirs, *weights)
    part_back = lax.ppermute(part_theirs, "core", swap)
    summed = (part_mine.astype(jnp.float32) + part_back.astype(jnp.float32)).astype(jnp.bfloat16)
    returned = lax.all_to_all(summed, chips, split_axis=0, concat_axis=0, tiled=True)
    attended = attend(queries, latent_cache, lengths)
    weight = jnp.sum(jnp.where(named, gates[:, :, None], 0.0), axis=1)
    weight = jnp.tile(weight, (1, columns))
    high = weight.astype(jnp.bfloat16)
    low = (weight - high.astype(jnp.float32)).astype(jnp.bfloat16)
    returned = returned.reshape(-1, width)
    moe_out = jnp.dot(high, returned, preferred_element_type=jnp.float32) + jnp.dot(
        low, returned, preferred_element_type=jnp.float32
    )
    return (moe_out.astype(jnp.bfloat16), attended)


def solution(mesh):
    devices = mesh.devices
    split = Mesh(devices.reshape(devices.shape[0] // 2, 2, 4, 4), ("y", "core", "x", "z"))
    attn, exp = ("y", "core"), ("x", "z")
    both = attn + exp
    placed = (
        P(both, None),
        P(both, None),
        P(both, None),
        P(exp, None, attn),
        P(exp, None, attn),
        P(exp, attn, None),
        P(both, None, None),
        P(both, None, None),
        P(both),
    )
    return jax.shard_map(
        body,
        mesh=split,
        in_specs=placed,
        out_specs=(P(both, None), P(both, None, None)),
        check_vma=False,
    )
```

time: 135 us -> 130 us (0.963)
  blocking collectives: 57.3 us -> 38.2 us
  matrix products: 21.5 us -> 38.5 us
  waiting for transfers between devices: 28.6 us -> 13.1 us
  local copies, waits for them, and re-layouts: 12 us -> 26.8 us
    all_to_all x1, blocking collectives: 57.3 us -> 38.2 us  [body(): lax.all_to_all(outgoing, chips, split_axis=0, concat_axis=0, tiled=True)]
    all_to_all x1, waiting for transfers between devices: 28.6 us -> 10.4 us  [body(): lax.all_to_all(summed, chips, split_axis=0, concat_axis=0, tiled=True)]
    dot_general x4 -> x7, matrix products: 4.6 us -> 21.6 us  [the longest x2 13.7 us: expert_slice(): out = jnp.dot(hidden, down_w, preferred_element_type=jnp.float32)]
    reshape x0 -> x4, local copies, waits for them, and re-layouts: none -> 17 us  [the longest x2 8.12 us: expert_slice(): rows = rows.reshape(-1, shape[-1])]
    reduce_sum x3 -> x1, other arithmetic: 6.9 us -> 0.09 us  [body(): selector = jnp.sum(named.astype(jnp.float32), axis=1).astype(jnp.bfloat16)]
    convert_element_type x0 -> x2, other arithmetic: none -> 5.77 us  [the longest x1 5.76 us: body(): (part_mine.astype(jnp.float32) + part_back.astype(jnp.float32)).astype(jn...]
    ppermute x0 -> x2, waiting for transfers between devices: none -> 2.67 us  [the longest x1 2.67 us: body(): theirs = lax.ppermute(mine, 'core', swap)]
    convert_element_type x2 -> x1, local copies, waits for them, and re-layouts: 5.93 us -> 5.51 us  [body(): part_mine.astype(jnp.float32) + part_back.astype(jnp.float32)]
  transfers between devices with their start and end apart: 1 -> 3, of which waited for: 1 -> 2; matrix products, arithmetic and copies ran while one was open for 13% -> 28% of each run, Pallas kernels for 0% -> 0%
where the time goes in v1:
time: 130 us; the launch traced here: 129 us
  matrix products  38.5 us (30%)
  blocking collectives  38.2 us (29%)
  local copies, waits for them, and re-layouts  26.8 us (21%)
  waiting for transfers between devices  13.1 us (10%)
  other arithmetic  6.24 us (5%)
  starting transfers between devices  5.93 us (5%)
    all_to_all x1, blocking collectives, body(): lax.all_to_all(outgoing, chips, split_axis=0, concat_axis=0, tiled=True)  38.2 us
    dot_general x2, matrix products, expert_slice(): out = jnp.dot(hidden, down_w, preferred_element_type=jnp.float32)  13.7 us
    all_to_all x1, waiting for transfers between devices, body(): lax.all_to_all(summed, chips, split_axis=0, concat_axis=0, tiled=True)  10.4 us
    sub x1, matrix products, attend(): exp_scores = jnp.where(visible, jnp.exp(scores - row_max), 0.0)  8.5 us
    dot_general x1, matrix products, attend(): jnp.einsum('rht,rtv->rhv', probs, values, preferred_element_type=jnp.floa...  8.36 us
    reshape x2, local copies, waits for them, and re-layouts, expert_slice(): rows = rows.reshape(-1, shape[-1])  8.12 us
    all_to_all x1, starting transfers between devices, body(): lax.all_to_all(summed, chips, split_axis=0, concat_axis=0, tiled=True)  5.79 us
    convert_element_type x1, other arithmetic, body(): (part_mine.astype(jnp.float32) + part_back.astype(jnp.float32)).astype(jn...  5.76 us
  transfers between devices with their start and end apart: 3, of which 2 were waited for; matrix products, arithmetic and copies ran while one was open for 28% of the time, Pallas kernels for 0%

profile of v1, /device:TPU:0, one launch (start us, length us, event | category | flops | bytes accessed | tf_op | source)
XLA Modules:
  0.0 129.5 jit_solution(4389502332737512501)
XLA Ops:
  0.6 0.8 copy.19
  1.7 0.2 select_reduce_fusion
  1.9 0.8 copy.21
  2.8 1.2 convolution_convert_fusion.2
  4.2 0.9 broadcast_in_dim.47
  5.2 38.2 %all_to_all.10 = bf16[64,2,7168]{2,1,0:T(2,128)(2,1)S(1)} all-to-all(bf16[64,2,7168]{2,1,0:T(2,128)(2,1)S(1)} %bitcast.38), channel_id=1, replica_groups=mesh['y'=4,'core'=2,'x'=4,'z'=4] {'y','x','z'}, dimensions={0} | all-to-all | bytes 3670016 | tf_op jit(solution)/shard_map/all_to_all | solution.py:60
  43.4 1.2 copy-done.1
  44.6 2.7 %collective-permute-done = bf16[64,2,7168]{2,1,0:T(2,128)(2,1)} collective-permute-done((bf16[64,2,7168]{2,1,0:T(2,128)(2,1)S(1)}, bf16[64,2,7168]{2,1,0:T(2,128)(2,1)}, u32[]{:S(2)}, u32[]{:S(2)}) %collective-permute-start) | collective-permute-done | bytes 1835040 | tf_op jit(solution)/shard_map/ppermute | solution.py:62
  47.3 4.1 %reshape.66 = bf16[128,7168]{1,0:T(8,128)(2,1)S(1)} reshape(bf16[64,2,7168]{2,1,0:T(2,128)(2,1)} %collective-permute-done) | data formatting | bytes 3670016 | tf_op jit(solution)/shard_map/reshape | solution.py:31
  51.3 2.7 %fusion.8 = f32[128,256]{1,0:T(8,128)S(1)} fusion(bf16[128,7168]{1,0:T(8,128)(2,1)S(1)} %reshape.66, bf16[1,7168,256]{2,1,0:T(8,128)(2,1)} %param.13), kind=kOutput, calls=%fused_computation.15 | convolution fusion | flops 469762048 | bytes 5636096 | tf_op jit(solution)/shard_map/dot_general | solution.py:33
  54.0 6.5 %convolution_convert_fusion = bf16[128,7168]{1,0:T(8,128)(2,1)} fusion(bf16[1,256,7168]{2,1,0:T(8,128)(2,1)} %param.14, f32[128,256]{1,0:T(8,128)S(1)} %fusion.8, bf16[128,7168]{1,0:T(8,128)(2,1)S(1)} %reshape.66, bf16[1,7168,256]{2,1,0:T(8,128)(2,1)} %param.12), kind=kOutput, calls=%fused_computation.1 | convolution fusion | flops 940638208 | bytes 11141120 | tf_op jit(solution)/shard_map/dot_general | solution.py:35
  60.6 4.8 %reshape.67 = bf16[64,2,7168]{2,1,0:T(2,128)(2,1)} reshape(bf16[128,7168]{1,0:T(8,128)(2,1)} %convolution_convert_fusion) | data formatting | bytes 3670016 | tf_op jit(solution)/shard_map/reshape | solution.py:36
  65.8 4.1 %reshape.65 = bf16[128,7168]{1,0:T(8,128)(2,1)S(1)} reshape(bf16[64,2,7168]{2,1,0:T(2,128)(2,1)} %copy-done.1) | data formatting | bytes 3670016 | tf_op jit(solution)/shard_map/reshape | solution.py:31
  69.9 2.7 %fusion.14 = f32[128,256]{1,0:T(8,128)S(1)} fusion(bf16[128,7168]{1,0:T(8,128)(2,1)S(1)} %reshape.65, bf16[1,7168,256]{2,1,0:T(8,128)(2,1)} %param.12), kind=kOutput, calls=%fused_computation.21 | convolution fusion | flops 469762048 | bytes 5636096 | tf_op jit(solution)/shard_map/dot_general | solution.py:32
  72.6 7.1 %fusion.1 = f32[128,7168]{1,0:T(8,128)} fusion(bf16[1,256,7168]{2,1,0:T(8,128)(2,1)} %param.14, bf16[128,7168]{1,0:T(8,128)(2,1)S(1)} %reshape.65, bf16[1,7168,256]{2,1,0:T(8,128)(2,1)} %param.13, f32[128,256]{1,0:T(8,128)S(1)} %fusion.14), kind=kOutput, calls=%fused_computation.3 | convolution fusion | flops 941555712 | bytes 12976128 | tf_op jit(solution)/shard_map/dot_general | solution.py:35
  79.7 5.5 %reshape.69 = f32[64,2,7168]{2,1,0:T(2,128)} reshape(f32[128,7168]{1,0:T(8,128)} %fusion.1) | data formatting | bytes 7340032 | tf_op jit(solution)/shard_map/convert_element_type | solution.py:67
  85.2 5.8 %add_convert_fusion = bf16[64,2,7168]{2,1,0:T(2,128)(2,1)} fusion(f32[64,2,7168]{2,1,0:T(2,128)} %reshape.69, bf16[64,2,7168]{2,1,0:T(2,128)(2,1)} %collective-permute-done.1), kind=kLoop, calls=%fused_computation.23 | loop fusion | flops 2752512 | bytes 7340032 | tf_op jit(solution)/shard_map/convert_element_type | solution.py:67
  91.0 5.8 %all-to-all-start.1 = ((bf16[64,2,7168]{2,1,0:T(2,128)(2,1)}), bf16[64,2,7168]{2,1,0:T(2,128)(2,1)}, u32[]{:S(2)}, u32[]{:S(2)}) async-start(bf16[64,2,7168]{2,1,0:T(2,128)(2,1)} %add_convert_fusion), calls=%async_computation.1 | async-start | bytes 3670016 | tf_op jit(solution)/shard_map/all_to_all | solution.py:68
  96.8 8.5 %fusion.48 = (f32[4,128]{1,0:T(4,128)S(1)}, f32[4,128,2048]{2,1,0:T(8,128)}) fusion(pred[4,2048]{1,0:T(4,128)(4,1)S(1)} %iota_compare_fusion, bf16[4,128,576]{1,2,0:T(8,128)(2,1)S(1)} %copy-done, bf16[4,2048,576]{1,2,0:T(8,128)(2,1)} %param.16), kind=kOutput, calls=%fused_computation.53 | convolution fusion | flops 1213204480 | bytes 14231552 | tf_op jit(solution)/shard_map/sub | solution.py:21
  105.3 8.4 %fusion.20 = bf16[4,128,512]{2,1,0:T(8,128)(2,1)} fusion(bf16[4,2048,576]{1,2,0:T(8,128)(2,1)} %param.16, f32[4,128,2048]{2,1,0:T(8,128)} %get-tuple-element.7, f32[4,128]{1,0:T(4,128)S(1)} %get-tuple-element.6), kind=kOutput, calls=%fused_computation.28 | convolution fusion | flops 1076101120 | bytes 13109248 | tf_op jit(solution)/shard_map/rht,rtv->rhv/dot_general | solution.py:24
  113.6 10.4 %all-to-all-done.1 = bf16[64,2,7168]{2,1,0:T(2,128)(2,1)} async-done(((bf16[64,2,7168]{2,1,0:T(2,128)(2,1)}), bf16[64,2,7168]{2,1,0:T(2,128)(2,1)}, u32[]{:S(2)}, u32[]{:S(2)}) %all-to-all-start.1) | async-done | bytes 1835040 | tf_op jit(solution)/shard_map/all_to_all | solution.py:68
  124.0 4.1 %reshape.68 = bf16[128,7168]{1,0:T(8,128)(2,1)S(1)} reshape(bf16[64,2,7168]{2,1,0:T(2,128)(2,1)} %all-to-all-done.1) | data formatting | bytes 3670016 | tf_op jit(solution)/shard_map/reshape | solution.py:74
  128.1 0.3 fusion.51
  128.5 1.0 fusion.4
  (21 shorter events, 1.0 us)
Async XLA Ops:
  0.6 96.1 %copy-start = (bf16[4,128,576]{1,2,0:T(8,128)(2,1)S(1)}, bf16[4,128,576]{1,2,0:T(8,128)(2,1)}, u32[]{:S(2)}) copy-start(bf16[4,128,576]{1,2,0:T(8,128)(2,1)} %param.15) | copy-start | bytes 1769476
  43.3 1.3 copy-start.1
  43.4 3.9 %collective-permute-start = (bf16[64,2,7168]{2,1,0:T(2,128)(2,1)S(1)}, bf16[64,2,7168]{2,1,0:T(2,128)(2,1)}, u32[]{:S(2)}, u32[]{:S(2)}) collective-permute-start(bf16[64,2,7168]{2,1,0:T(2,128)(2,1)S(1)} %all_to_all.10), channel_id=1, source_target_pairs={{0,16},{16,0},{1,17},{17,1},{2,18},{18,2},{3,19},{19,3},{4,20},{20... | collective-permute-start | bytes 5505032 | tf_op jit(solution)/shard_map/ppermute | solution.py:62
  60.6 5.1 %copy-start.2 = (s32[4]{0:T(128)S(1)}, s32[4]{0:T(128)}, u32[]{:S(2)}) copy-start(s32[4]{0:T(128)} %param.17) | copy-start | bytes 52
  65.4 19.8 %collective-permute-start.1 = (bf16[64,2,7168]{2,1,0:T(2,128)(2,1)}, bf16[64,2,7168]{2,1,0:T(2,128)(2,1)}, u32[]{:S(2)}, u32[]{:S(2)}) collective-permute-start(bf16[64,2,7168]{2,1,0:T(2,128)(2,1)} %reshape.67), channel_id=1, source_target_pairs={{0,16},{16,0},{1,17},{17,1},{2,18},{18,2},{3,19},{19,3},{4,20},{20... | collective-permute-start | bytes 5505032 | tf_op jit(solution)/shard_map/ppermute | solution.py:66
  91.0 33.1 %all-to-all-start.1 = ((bf16[64,2,7168]{2,1,0:T(2,128)(2,1)}), bf16[64,2,7168]{2,1,0:T(2,128)(2,1)}, u32[]{:S(2)}, u32[]{:S(2)}) async-start(bf16[64,2,7168]{2,1,0:T(2,128)(2,1)} %add_convert_fusion), calls=%async_computation.1 | async-start | bytes 3670016 | tf_op jit(solution)/shard_map/all_to_all | solution.py:68

commit v2 on v1

--- a/solution.py
+++ b/solution.py
@@ -1,6 +1,8 @@
 import jax
 import jax.numpy as jnp
 from jax import lax
+from jax.experimental import pallas as pl
+from jax.experimental.pallas import tpu as pltpu
 from jax.sharding import Mesh, PartitionSpec as P
 
 KV = 512
@@ -26,21 +28,97 @@
     )
 
 
-def expert_slice(rows, gate_w, up_w, down_w):
-    shape = rows.shape
-    rows = rows.reshape(-1, shape[-1])
-    gate_act = jnp.dot(rows, gate_w, preferred_element_type=jnp.float32)
-    up_act = jnp.dot(rows, up_w, preferred_element_type=jnp.float32)
-    hidden = (jax.nn.silu(gate_act) * up_act).astype(jnp.bfloat16)
-    out = jnp.dot(hidden, down_w, preferred_element_type=jnp.float32)
-    return out.astype(jnp.bfloat16).reshape(shape)
+STEPS = 7
+
+
+def expert_kernel(*refs):
+    blocks, refs = refs[:8], refs[8:]
+    gate_hbm, up_hbm, down_hbm, theirs_ref, mine_ref = refs[:5]
+    gate_buf, up_buf, down_buf, gate_acc, up_acc, sems = refs[5:]
+    depth = gate_hbm.shape[1] // STEPS
+
+    def part(step):
+        return pl.ds(step * depth, depth)
+
+    def gate_copy(step):
+        return pltpu.make_async_copy(
+            gate_hbm.at[0, part(step), :], gate_buf.at[part(step), :], sems.at[0, step]
+        )
+
+    def up_copy(step):
+        return pltpu.make_async_copy(
+            up_hbm.at[0, part(step), :], up_buf.at[part(step), :], sems.at[1, step]
+        )
+
+    def down_copy(step):
+        return pltpu.make_async_copy(
+            down_hbm.at[0, :, part(step)], down_buf.at[:, part(step)], sems.at[2, step]
+        )
+
+    for step in range(STEPS):
+        gate_copy(step).start()
+        up_copy(step).start()
+    for step in range(STEPS):
+        down_copy(step).start()
+    for step in range(STEPS):
+        rows = jnp.concatenate([b[:, part(step)] for b in blocks], axis=0)
+        gate_copy(step).wait()
+        gate_act = jnp.dot(rows, gate_buf[part(step), :], preferred_element_type=jnp.float32)
+        up_copy(step).wait()
+        up_act = jnp.dot(rows, up_buf[part(step), :], preferred_element_type=jnp.float32)
+        if step == 0:
+            gate_acc[...] = gate_act
+            up_acc[...] = up_act
+        else:
+            gate_acc[...] += gate_act
+            up_acc[...] += up_act
+    gate_act = gate_acc[...]
+    hidden = (gate_act / (1.0 + jnp.exp(-gate_act)) * up_acc[...]).astype(jnp.bfloat16)
+    half = hidden.shape[0] // 2
+    for step in range(STEPS):
+        down_copy(step).wait()
+        out = jnp.dot(hidden, down_buf[:, part(step)], preferred_element_type=jnp.float32)
+        out = out.astype(jnp.bfloat16)
+        theirs_ref[:, part(step)] = out[:half]
+        mine_ref[:, part(step)] = out[half:]
+
+
+def experts_on(theirs, mine, gate_w, up_w, down_w):
+    rows, width = mine[0].shape
+    hidden = gate_w.shape[2]
+    half = jax.ShapeDtypeStruct((len(mine) * rows, width), jnp.bfloat16)
+    total = 2 * len(mine) * rows
+    whole = pl.BlockSpec(memory_space=pltpu.VMEM)
+    return pl.pallas_call(
+        expert_kernel,
+        out_shape=(half, half),
+        in_specs=[whole] * 8 + [pl.BlockSpec(memory_space=pl.ANY)] * 3,
+        out_specs=(whole, whole),
+        scratch_shapes=[
+            pltpu.VMEM((width, hidden), jnp.bfloat16),
+            pltpu.VMEM((width, hidden), jnp.bfloat16),
+            pltpu.VMEM((hidden, width), jnp.bfloat16),
+            pltpu.VMEM((total, hidden), jnp.float32),
+            pltpu.VMEM((total, hidden), jnp.float32),
+            pltpu.SemaphoreType.DMA((3, STEPS)),
+        ],
+        compiler_params=pltpu.CompilerParams(vmem_limit_bytes=40 * 2**20),
+        cost_estimate=pl.CostEstimate(
+            flops=6 * total * width * hidden,
+            bytes_accessed=6 * width * hidden,
+            transcendentals=total * hidden,
+        ),
+    )(*theirs, *mine, gate_w, up_w, down_w)
+
+
+def shift(size, by):
+    return [(i, (i + by) % size) for i in range(size)]
 
 
 def body(moe_in, routes, gates, gate_w, up_w, down_w, queries, latent_cache, lengths):
     rows_here, top_count = routes.shape
     experts = lax.axis_size("x") * lax.axis_size("z")
     columns = lax.axis_size("y")
-    chips = ("y", "x", "z")
     width = moe_in.shape[1]
     capacity = 2
     flat_routes = routes.reshape(-1)
@@ -54,21 +132,31 @@
     named = targets[:, :, None] == places[None, None, :]
     selector = jnp.sum(named.astype(jnp.float32), axis=1).astype(jnp.bfloat16)
     outgoing = jnp.dot(selector.T, moe_in, preferred_element_type=jnp.float32).astype(jnp.bfloat16)
-    outgoing = outgoing.reshape(1, experts, capacity, width)
-    outgoing = jnp.broadcast_to(outgoing, (columns, experts, capacity, width))
-    outgoing = outgoing.reshape(columns * experts, capacity, width)
-    mine = lax.all_to_all(outgoing, chips, split_axis=0, concat_axis=0, tiled=True)
-    swap = [(0, 1), (1, 0)]
-    theirs = lax.ppermute(mine, "core", swap)
-    weights = (gate_w[0], up_w[0], down_w[0])
-    part_mine = expert_slice(mine, *weights)
-    part_theirs = expert_slice(theirs, *weights)
-    part_back = lax.ppermute(part_theirs, "core", swap)
-    summed = (part_mine.astype(jnp.float32) + part_back.astype(jnp.float32)).astype(jnp.bfloat16)
-    returned = lax.all_to_all(summed, chips, split_axis=0, concat_axis=0, tiled=True)
+    outgoing = outgoing.reshape(experts, capacity, width)
+    own = lax.all_to_all(outgoing, ("x", "z"), split_axis=0, concat_axis=0, tiled=True)
+    own = own.reshape(experts * capacity, width)
+    steps = [by for by in (2, 1, 3) if by < columns]
+    mine = [own] + [lax.ppermute(own, "y", shift(columns, by)) for by in steps]
+    theirs = [lax.ppermute(block, "core", shift(2, 1)) for block in mine]
+    part_theirs, part_mine = experts_on(theirs, mine, gate_w, up_w, down_w)
+    part_back = lax.ppermute(part_theirs, "core", shift(2, 1))
+    summed = [
+        (
+            part_mine[i * own.shape[0] : (i + 1) * own.shape[0]].astype(jnp.float32)
+            + part_back[i * own.shape[0] : (i + 1) * own.shape[0]].astype(jnp.float32)
+        ).astype(jnp.bfloat16)
+        for i in range(columns)
+    ]
+    arrived = [
+        lax.ppermute(block, "y", shift(columns, -by)) for block, by in zip(summed[1:], steps)
+    ]
+    total = summed[0].astype(jnp.float32)
+    for block in arrived:
+        total = total + block.astype(jnp.float32)
+    total = total.astype(jnp.bfloat16).reshape(experts, capacity, width)
+    returned = lax.all_to_all(total, ("x", "z"), split_axis=0, concat_axis=0, tiled=True)
     attended = attend(queries, latent_cache, lengths)
     weight = jnp.sum(jnp.where(named, gates[:, :, None], 0.0), axis=1)
-    weight = jnp.tile(weight, (1, columns))
     high = weight.astype(jnp.bfloat16)
     low = (weight - high.astype(jnp.float32)).astype(jnp.bfloat16)
     returned = returned.reshape(-1, width)

time: 130 us -> 107 us (0.82)
  waiting for transfers between devices: 13.1 us -> 34.4 us
  local copies, waits for them, and re-layouts: 26.8 us -> 6.56 us
  blocking collectives: 38.2 us -> 18.6 us
  matrix products: 38.5 us -> 19.1 us
  starting transfers between devices: 5.93 us -> 15.8 us
  Pallas kernels: 0 us -> 7.78 us
  other arithmetic: 6.24 us -> 3.3 us
    ppermute x2 -> x11, waiting for transfers between devices: 2.67 us -> 32.5 us  [the longest x3 16 us: body(): mine = [own] + [lax.ppermute(own, 'y', shift(columns, by)) for by in steps]]
    all_to_all x1, blocking collectives: 38.2 us -> 18.6 us  [body(): lax.all_to_all(outgoing, ('x', 'z'), split_axis=0, concat_axis=0, tiled=T...]
    dot_general x4 -> x0, matrix products: 19 us -> none  [the longest x2 13.7 us: expert_slice(): out = jnp.dot(hidden, down_w, preferred_element_type=jnp.float32)]
    ppermute x2 -> x11, starting transfers between devices: 0.14 us -> 11.9 us  [the longest x3 6.51 us: body(): mine = [own] + [lax.ppermute(own, 'y', shift(columns, by)) for by in steps]]
    reshape x3, local copies, waits for them, and re-layouts: 12.9 us -> 1.29 us  [the longest x1 0.94 us: body(): total = total.astype(jnp.bfloat16).reshape(experts, capacity, width)]
    all_to_all x1, waiting for transfers between devices: 10.4 us -> 1.85 us  [body(): lax.all_to_all(total, ('x', 'z'), split_axis=0, concat_axis=0, tiled=True)]
    pallas_call x0 -> x1, Pallas kernels: none -> 7.78 us  [experts_on(): pl.pallas_call(expert_kernel, out_shape=(half, half), in_specs=[whole] *...]
    convert_element_type x1 -> x0, local copies, waits for them, and re-layouts: 5.51 us -> none  [body(): part_mine.astype(jnp.float32) + part_back.astype(jnp.float32)]
  transfers between devices with their start and end apart: 3 -> 12, of which waited for: 2 -> 9; matrix products, arithmetic and copies ran while one was open for 28% -> 16% of each run, Pallas kernels for 0% -> 0%
where the time goes in v2:
time: 107 us; the launch traced here: 106 us
  waiting for transfers between devices  34.4 us (32%)
  matrix products  19.1 us (18%)
  blocking collectives  18.6 us (17%)
  starting transfers between devices  15.8 us (15%)
  Pallas kernels  7.78 us (7%)
  local copies, waits for them, and re-layouts  6.56 us (6%)
  other arithmetic  3.3 us (3%)
    all_to_all x1, blocking collectives, body(): lax.all_to_all(outgoing, ('x', 'z'), split_axis=0, concat_axis=0, tiled=T...  18.6 us
    ppermute x3, waiting for transfers between devices, body(): mine = [own] + [lax.ppermute(own, 'y', shift(columns, by)) for by in steps]  16 us
    ppermute x3, waiting for transfers between devices, body(): lax.ppermute(block, 'y', shift(columns, -by))  11 us
    sub x1, matrix products, attend(): exp_scores = jnp.where(visible, jnp.exp(scores - row_max), 0.0)  8.53 us
    dot_general x1, matrix products, attend(): jnp.einsum('rht,rtv->rhv', probs, values, preferred_element_type=jnp.floa...  8.36 us
    pallas_call x1, Pallas kernels, experts_on(): pl.pallas_call(expert_kernel, out_shape=(half, half), in_specs=[whole] *...  7.78 us
    ppermute x3, starting transfers between devices, body(): mine = [own] + [lax.ppermute(own, 'y', shift(columns, by)) for by in steps]  6.51 us
    ppermute x3, starting transfers between devices, body(): lax.ppermute(block, 'y', shift(columns, -by))  5.04 us
  transfers between devices with their start and end apart: 12, of which 9 were waited for; matrix products, arithmetic and copies ran while one was open for 16% of the time, Pallas kernels for 0%

profile of v2, /device:TPU:0, one launch (start us, length us, event | category | flops | bytes accessed | tf_op | source)
XLA Modules:
  0.0 106.1 jit_solution(13006216750425635851)
XLA Ops:
  0.6 0.8 copy.19
  2.8 1.2 %convolution_convert_fusion = bf16[32,7168]{1,0:T(8,128)(2,1)S(1)} fusion(bf16[6,7168]{1,0:T(8,128)(2,1)} %param.9, bf16[6,32]{1,0:T(8,128)(2,1)S(1)} %get-tuple-element.7), kind=kOutput, calls=%fused_computation.3 | convolution fusion | flops 2981888 | bytes 545152 | tf_op jit(solution)/shard_map/dot_general | solution.py:134
  4.2 18.6 %all_to_all.10 = bf16[16,2,7168]{2,1,0:T(2,128)(2,1)S(1)} all-to-all(bf16[16,2,7168]{2,1,0:T(2,128)(2,1)S(1)} %reshape.48), channel_id=1, replica_groups=mesh['y'=4,'core'=2,'x'=4,'z'=4] {'x','z'}, dimensions={0} | all-to-all | bytes 917504 | tf_op jit(solution)/shard_map/all_to_all | solution.py:136
  22.9 3.3 %collective-permute-start.1 = (bf16[32,7168]{1,0:T(8,128)(2,1)S(1)}, bf16[32,7168]{1,0:T(8,128)(2,1)S(1)}, u32[]{:S(2)}, u32[]{:S(2)}) collective-permute-start(bf16[32,7168]{1,0:T(8,128)(2,1)S(1)} %reshape.49.refs_4_), channel_id=1, source_target_pairs={{0,64},{32,96},{64,0},{96,32},{1,65},{33,97},{65,1},{97,33},{2,66}... | collective-permute-start | bytes 1376264 | tf_op jit(solution)/shard_map/ppermute | solution.py:139
  26.9 2.6 %collective-permute-start.5 = (bf16[32,7168]{1,0:T(8,128)(2,1)S(1)}, bf16[32,7168]{1,0:T(8,128)(2,1)S(1)}, u32[]{:S(2)}, u32[]{:S(2)}) collective-permute-start(bf16[32,7168]{1,0:T(8,128)(2,1)S(1)} %reshape.49.refs_4_), channel_id=1, source_target_pairs={{0,96},{32,0},{64,32},{96,64},{1,97},{33,1},{65,33},{97,65},{2,98}... | collective-permute-start | bytes 1376264 | tf_op jit(solution)/shard_map/ppermute | solution.py:139
  29.5 8.6 %collective-permute-done.1.refs_5_ = bf16[32,7168]{1,0:T(8,128)(2,1)S(1)} collective-permute-done((bf16[32,7168]{1,0:T(8,128)(2,1)S(1)}, bf16[32,7168]{1,0:T(8,128)(2,1)S(1)}, u32[]{:S(2)}, u32[]{:S(2)}) %collective-permute-start.1) | collective-permute-done | bytes 458784 | tf_op jit(solution)/shard_map/ppermute | solution.py:139
  38.0 7.1 %collective-permute-done.3.refs_6_ = bf16[32,7168]{1,0:T(8,128)(2,1)S(1)} collective-permute-done((bf16[32,7168]{1,0:T(8,128)(2,1)S(1)}, bf16[32,7168]{1,0:T(8,128)(2,1)S(1)}, u32[]{:S(2)}, u32[]{:S(2)}) %collective-permute-start.3) | collective-permute-done | bytes 458784 | tf_op jit(solution)/shard_map/ppermute | solution.py:139
  45.6 1.3 %collective-permute-done.4.refs_2_ = bf16[32,7168]{1,0:T(8,128)(2,1)S(1)} collective-permute-done((bf16[32,7168]{1,0:T(8,128)(2,1)S(1)}, bf16[32,7168]{1,0:T(8,128)(2,1)S(1)}, u32[]{:S(2)}, u32[]{:S(2)}) %collective-permute-start.4) | collective-permute-done | bytes 458784 | tf_op jit(solution)/shard_map/ppermute | solution.py:140
  47.6 2.0 %copy-done.1 = bf16[1,7168,256]{2,1,0:T(8,128)(2,1)S(1)} copy-done((bf16[1,7168,256]{2,1,0:T(8,128)(2,1)S(1)}, bf16[1,7168,256]{2,1,0:T(8,128)(2,1)}, u32[]{:S(2)}) %copy-start.1) | copy-done | bytes 3670040
  49.6 7.8 %shard_map.104 = (bf16[128,7168]{1,0:T(8,128)(2,1)S(1)}, bf16[128,7168]{1,0:T(8,128)(2,1)S(1)}) custom-call(bf16[32,7168]{1,0:T(8,128)(2,1)S(1)} %collective-permute-done.refs_0_, bf16[32,7168]{1,0:T(8,128)(2,1)S(1)} %collective-permute-done.2.refs_1_, bf16[32,7168]{1,0:T(8,128)(2,1)S(1)} %collective-permute-done.4.refs_2_, ...), custom_call_target="tpu_custom_call" | custom-call | flops 2818572288 | bytes 11010048 | tf_op jit(solution)/shard_map/pallas_call | solution.py:92
  57.7 3.6 %collective-permute-done.7 = bf16[128,7168]{1,0:T(8,128)(2,1)S(1)} collective-permute-done((bf16[128,7168]{1,0:T(8,128)(2,1)S(1)}, bf16[128,7168]{1,0:T(8,128)(2,1)S(1)}, u32[]{:S(2)}, u32[]{:S(2)}) %collective-permute-start.7) | collective-permute-done | bytes 1835040 | tf_op jit(solution)/shard_map/ppermute | solution.py:142
  61.3 1.3 %copy-done.2 = bf16[128,7168]{1,0:T(8,128)(2,1)} copy-done((bf16[128,7168]{1,0:T(8,128)(2,1)}, bf16[128,7168]{1,0:T(8,128)(2,1)S(1)}, u32[]{:S(2)}) %copy-start.2) | copy-done | bytes 1835032
  62.6 1.3 %add_convert_fusion.3 = (bf16[32,7168]{1,0:T(8,128)(2,1)}, bf16[32,7168]{1,0:T(8,128)(2,1)}, bf16[32,7168]{1,0:T(8,128)(2,1)S(1)}) fusion(bf16[128,7168]{1,0:T(8,128)(2,1)S(1)} %collective-permute-done.7, bf16[128,7168]{1,0:T(8,128)(2,1)S(1)} %get-tuple-element.4), kind=kLoop, calls=%fused_computation.18 | loop fusion | flops 2752512 | bytes 4128768 | tf_op jit(solution)/shard_map/convert_element_type | solution.py:147
  63.8 1.7 %collective-permute-start.10 = (bf16[32,7168]{1,0:T(8,128)(2,1)}, bf16[32,7168]{1,0:T(8,128)(2,1)S(1)}, u32[]{:S(2)}, u32[]{:S(2)}) collective-permute-start(bf16[32,7168]{1,0:T(8,128)(2,1)} %get-tuple-element.9), channel_id=1, source_target_pairs={{0,32},{32,64},{64,96},{96,0},{1,33},{33,65},{65,97},{97,1},{2,34}... | collective-permute-start | bytes 1376264 | tf_op jit(solution)/shard_map/ppermute | solution.py:151
  65.5 2.1 %collective-permute-start.8 = (bf16[32,7168]{1,0:T(8,128)(2,1)}, bf16[32,7168]{1,0:T(8,128)(2,1)}, u32[]{:S(2)}, u32[]{:S(2)}) collective-permute-start(bf16[32,7168]{1,0:T(8,128)(2,1)} %get-tuple-element.8), channel_id=1, source_target_pairs={{0,64},{32,96},{64,0},{96,32},{1,65},{33,97},{65,1},{97,33},{2,66}... | collective-permute-start | bytes 1376264 | tf_op jit(solution)/shard_map/ppermute | solution.py:151
  67.6 1.2 %collective-permute-start.9 = (bf16[32,7168]{1,0:T(8,128)(2,1)S(1)}, bf16[32,7168]{1,0:T(8,128)(2,1)}, u32[]{:S(2)}, u32[]{:S(2)}) collective-permute-start(bf16[32,7168]{1,0:T(8,128)(2,1)S(1)} %get-tuple-element.10), channel_id=1, source_target_pairs={{0,96},{32,0},{64,32},{96,64},{1,97},{33,1},{65,33},{97,65},{2,98}... | collective-permute-start | bytes 1376264 | tf_op jit(solution)/shard_map/ppermute | solution.py:151
  68.9 8.5 %fusion.19 = (f32[4,128]{1,0:T(4,128)S(1)}, f32[4,128,2048]{2,1,0:T(8,128)}) fusion(pred[4,2048]{1,0:T(4,128)(4,1)S(1)} %iota_compare_fusion, bf16[4,128,576]{1,2,0:T(8,128)(2,1)S(1)} %copy-done, bf16[4,2048,576]{1,2,0:T(8,128)(2,1)} %param.16), kind=kOutput, calls=%fused_computation.35 | convolution fusion | flops 1213204480 | bytes 14231552 | tf_op jit(solution)/shard_map/sub | solution.py:23
  78.0 10.3 %collective-permute-done.8 = bf16[32,7168]{1,0:T(8,128)(2,1)} collective-permute-done((bf16[32,7168]{1,0:T(8,128)(2,1)}, bf16[32,7168]{1,0:T(8,128)(2,1)}, u32[]{:S(2)}, u32[]{:S(2)}) %collective-permute-start.8) | collective-permute-done | bytes 458784 | tf_op jit(solution)/shard_map/ppermute | solution.py:151
  88.4 1.6 %add_convert_fusion = bf16[32,7168]{1,0:T(8,128)(2,1)S(1)} fusion(bf16[32,7168]{1,0:T(8,128)(2,1)S(1)} %collective-permute-done.10, bf16[32,7168]{1,0:T(8,128)(2,1)} %collective-permute-done.9, bf16[32,7168]{1,0:T(8,128)(2,1)} %collective-permute-done.8, bf16[128,7168]{1,0:T(8,128)(2,1)} %copy-done.2, bf16[128,7168]{1,0:T(8,128)(2,1)S(1)} %get-tuple-element.4), kind=kLoop, calls=%fused_computation.15 | loop fusion | flops 2752512 | bytes 2752512 | tf_op jit(solution)/shard_map/convert_element_type | solution.py:156
  89.9 0.9 reshape.50
  90.9 3.9 %all-to-all-start.1 = ((bf16[16,2,7168]{2,1,0:T(2,128)(2,1)}), bf16[16,2,7168]{2,1,0:T(2,128)(2,1)S(1)}, u32[]{:S(2)}, u32[]{:S(2)}) async-start(bf16[16,2,7168]{2,1,0:T(2,128)(2,1)} %reshape.50), calls=%async_computation.1 | async-start | bytes 917504 | tf_op jit(solution)/shard_map/all_to_all | solution.py:157
  94.7 8.4 %fusion.9 = bf16[4,128,512]{2,1,0:T(8,128)(2,1)} fusion(bf16[4,2048,576]{1,2,0:T(8,128)(2,1)} %param.16, f32[4,128,2048]{2,1,0:T(8,128)} %get-tuple-element.12, f32[4,128]{1,0:T(4,128)S(1)} %get-tuple-element.11), kind=kOutput, calls=%fused_computation.14 | convolution fusion | flops 1076101120 | bytes 13109248 | tf_op jit(solution)/shard_map/rht,rtv->rhv/dot_general | solution.py:26
  103.1 1.9 %all-to-all-done.1 = bf16[16,2,7168]{2,1,0:T(2,128)(2,1)S(1)} async-done(((bf16[16,2,7168]{2,1,0:T(2,128)(2,1)}), bf16[16,2,7168]{2,1,0:T(2,128)(2,1)S(1)}, u32[]{:S(2)}, u32[]{:S(2)}) %all-to-all-start.1) | async-done | bytes 458784 | tf_op jit(solution)/shard_map/all_to_all | solution.py:157
  105.3 0.8 fusion.3
  (31 shorter events, 4.9 us)
Async XLA Ops:
  0.6 68.2 %copy-start = (bf16[4,128,576]{1,2,0:T(8,128)(2,1)S(1)}, bf16[4,128,576]{1,2,0:T(8,128)(2,1)}, u32[]{:S(2)}) copy-start(bf16[4,128,576]{1,2,0:T(8,128)(2,1)} %param.15) | copy-start | bytes 1769476
  22.8 34.9 %copy-start.3 = (s32[4]{0:T(128)S(1)}, s32[4]{0:T(128)}, u32[]{:S(2)}) copy-start(s32[4]{0:T(128)} %param.17) | copy-start | bytes 52
  22.9 15.1 %collective-permute-start.1 = (bf16[32,7168]{1,0:T(8,128)(2,1)S(1)}, bf16[32,7168]{1,0:T(8,128)(2,1)S(1)}, u32[]{:S(2)}, u32[]{:S(2)}) collective-permute-start(bf16[32,7168]{1,0:T(8,128)(2,1)S(1)} %reshape.49.refs_4_), channel_id=1, source_target_pairs={{0,64},{32,96},{64,0},{96,32},{1,65},{33,97},{65,1},{97,33},{2,66}... | collective-permute-start | bytes 1376264 | tf_op jit(solution)/shard_map/ppermute | solution.py:139
  26.2 18.9 %collective-permute-start.3 = (bf16[32,7168]{1,0:T(8,128)(2,1)S(1)}, bf16[32,7168]{1,0:T(8,128)(2,1)S(1)}, u32[]{:S(2)}, u32[]{:S(2)}) collective-permute-start(bf16[32,7168]{1,0:T(8,128)(2,1)S(1)} %reshape.49.refs_4_), channel_id=1, source_target_pairs={{0,32},{32,64},{64,96},{96,0},{1,33},{33,65},{65,97},{97,1},{2,34}... | collective-permute-start | bytes 1376264 | tf_op jit(solution)/shard_map/ppermute | solution.py:139
  26.9 18.6 %collective-permute-start.5 = (bf16[32,7168]{1,0:T(8,128)(2,1)S(1)}, bf16[32,7168]{1,0:T(8,128)(2,1)S(1)}, u32[]{:S(2)}, u32[]{:S(2)}) collective-permute-start(bf16[32,7168]{1,0:T(8,128)(2,1)S(1)} %reshape.49.refs_4_), channel_id=1, source_target_pairs={{0,96},{32,0},{64,32},{96,64},{1,97},{33,1},{65,33},{97,65},{2,98}... | collective-permute-start | bytes 1376264 | tf_op jit(solution)/shard_map/ppermute | solution.py:139
  29.5 16.2 %collective-permute-start = (bf16[32,7168]{1,0:T(8,128)(2,1)S(1)}, bf16[32,7168]{1,0:T(8,128)(2,1)S(1)}, u32[]{:S(2)}, u32[]{:S(2)}) collective-permute-start(bf16[32,7168]{1,0:T(8,128)(2,1)S(1)} %reshape.49.refs_4_), channel_id=1, source_target_pairs={{0,16},{16,0},{1,17},{17,1},{2,18},{18,2},{3,19},{19,3},{4,20},{20... | collective-permute-start | bytes 1376264 | tf_op jit(solution)/shard_map/ppermute | solution.py:140
  38.0 7.6 %collective-permute-start.2 = (bf16[32,7168]{1,0:T(8,128)(2,1)S(1)}, bf16[32,7168]{1,0:T(8,128)(2,1)S(1)}, u32[]{:S(2)}, u32[]{:S(2)}) collective-permute-start(bf16[32,7168]{1,0:T(8,128)(2,1)S(1)} %collective-permute-done.1.refs_5_), channel_id=1, source_target_pairs={{0,16},{16,0},{1,17},{17,1},{2,18},{18,2},{3,19},{19,3},{4,20},{20... | collective-permute-start | bytes 1376264 | tf_op jit(solution)/shard_map/ppermute | solution.py:140
  45.1 1.8 %collective-permute-start.4 = (bf16[32,7168]{1,0:T(8,128)(2,1)S(1)}, bf16[32,7168]{1,0:T(8,128)(2,1)S(1)}, u32[]{:S(2)}, u32[]{:S(2)}) collective-permute-start(bf16[32,7168]{1,0:T(8,128)(2,1)S(1)} %collective-permute-done.3.refs_6_), channel_id=1, source_target_pairs={{0,16},{16,0},{1,17},{17,1},{2,18},{18,2},{3,19},{19,3},{4,20},{20... | collective-permute-start | bytes 1376264 | tf_op jit(solution)/shard_map/ppermute | solution.py:140
  45.5 2.1 %collective-permute-start.6 = (bf16[32,7168]{1,0:T(8,128)(2,1)S(1)}, bf16[32,7168]{1,0:T(8,128)(2,1)S(1)}, u32[]{:S(2)}, u32[]{:S(2)}) collective-permute-start(bf16[32,7168]{1,0:T(8,128)(2,1)S(1)} %collective-permute-done.5.refs_7_), channel_id=1, source_target_pairs={{0,16},{16,0},{1,17},{17,1},{2,18},{18,2},{3,19},{19,3},{4,20},{20... | collective-permute-start | bytes 1376264 | tf_op jit(solution)/shard_map/ppermute | solution.py:140
  47.6 2.0 %copy-start.1 = (bf16[1,7168,256]{2,1,0:T(8,128)(2,1)S(1)}, bf16[1,7168,256]{2,1,0:T(8,128)(2,1)}, u32[]{:S(2)}) copy-start(bf16[1,7168,256]{2,1,0:T(8,128)(2,1)} %refs_8_.1) | copy-start | bytes 11010052
  57.4 3.9 %collective-permute-start.7 = (bf16[128,7168]{1,0:T(8,128)(2,1)S(1)}, bf16[128,7168]{1,0:T(8,128)(2,1)S(1)}, u32[]{:S(2)}, u32[]{:S(2)}) collective-permute-start(bf16[128,7168]{1,0:T(8,128)(2,1)S(1)} %get-tuple-element.5), channel_id=1, source_target_pairs={{0,16},{16,0},{1,17},{17,1},{2,18},{18,2},{3,19},{19,3},{4,20},{20... | collective-permute-start | bytes 5505032 | tf_op jit(solution)/shard_map/ppermute | solution.py:142
  61.3 1.3 %copy-start.2 = (bf16[128,7168]{1,0:T(8,128)(2,1)}, bf16[128,7168]{1,0:T(8,128)(2,1)S(1)}, u32[]{:S(2)}) copy-start(bf16[128,7168]{1,0:T(8,128)(2,1)S(1)} %collective-permute-done.7) | copy-start | bytes 5505028
  63.8 14.2 %collective-permute-start.10 = (bf16[32,7168]{1,0:T(8,128)(2,1)}, bf16[32,7168]{1,0:T(8,128)(2,1)S(1)}, u32[]{:S(2)}, u32[]{:S(2)}) collective-permute-start(bf16[32,7168]{1,0:T(8,128)(2,1)} %get-tuple-element.9), channel_id=1, source_target_pairs={{0,32},{32,64},{64,96},{96,0},{1,33},{33,65},{65,97},{97,1},{2,34}... | collective-permute-start | bytes 1376264 | tf_op jit(solution)/shard_map/ppermute | solution.py:151
  65.5 22.8 %collective-permute-start.8 = (bf16[32,7168]{1,0:T(8,128)(2,1)}, bf16[32,7168]{1,0:T(8,128)(2,1)}, u32[]{:S(2)}, u32[]{:S(2)}) collective-permute-start(bf16[32,7168]{1,0:T(8,128)(2,1)} %get-tuple-element.8), channel_id=1, source_target_pairs={{0,64},{32,96},{64,0},{96,32},{1,65},{33,97},{65,1},{97,33},{2,66}... | collective-permute-start | bytes 1376264 | tf_op jit(solution)/shard_map/ppermute | solution.py:151
  67.6 20.7 %collective-permute-start.9 = (bf16[32,7168]{1,0:T(8,128)(2,1)S(1)}, bf16[32,7168]{1,0:T(8,128)(2,1)}, u32[]{:S(2)}, u32[]{:S(2)}) collective-permute-start(bf16[32,7168]{1,0:T(8,128)(2,1)S(1)} %get-tuple-element.10), channel_id=1, source_target_pairs={{0,96},{32,0},{64,32},{96,64},{1,97},{33,1},{65,33},{97,65},{2,98}... | collective-permute-start | bytes 1376264 | tf_op jit(solution)/shard_map/ppermute | solution.py:151
  90.9 14.1 %all-to-all-start.1 = ((bf16[16,2,7168]{2,1,0:T(2,128)(2,1)}), bf16[16,2,7168]{2,1,0:T(2,128)(2,1)S(1)}, u32[]{:S(2)}, u32[]{:S(2)}) async-start(bf16[16,2,7168]{2,1,0:T(2,128)(2,1)} %reshape.50), calls=%async_computation.1 | async-start | bytes 917504 | tf_op jit(solution)/shard_map/all_to_all | solution.py:157

commit v3 on v1

v3 whole, which is shorter than its diff:
```python
import jax
import jax.numpy as jnp
from jax import lax
from jax.experimental import pallas as pl
from jax.experimental.pallas import tpu as pltpu
from jax.sharding import Mesh, PartitionSpec as P

KV = 512
CAP = 2
SLOTS = 32
SCORE_SCALE = 192.0 ** (-0.5)
LOG2_E = 1.4426950408889634
VMEM = pl.BlockSpec(memory_space=pltpu.VMEM)
SMALL = pl.CostEstimate(flops=1000, bytes_accessed=1000, transcendentals=0)


def slot_table(routes, experts):
    rows = routes.shape[1]
    shape = (experts * CAP, rows)
    expert = lax.broadcasted_iota(jnp.int32, shape, 0) // CAP
    first = routes[0:1, :] == expert
    second = routes[1:2, :] == expert
    named = (first | second).astype(jnp.float32)
    before = lax.broadcasted_iota(jnp.int32, (rows, rows), 0)
    after = lax.broadcasted_iota(jnp.int32, (rows, rows), 1)
    earlier = jnp.dot(named, (before < after).astype(jnp.float32), preferred_element_type=jnp.float32)
    slot = (lax.broadcasted_iota(jnp.int32, shape, 0) % CAP).astype(jnp.float32)
    here = (earlier > slot - 0.5) & (earlier < slot + 0.5)
    return first & here, second & here


def send_kernel(routes_ref, rows_ref, out_ref):
    first, second = slot_table(routes_ref[...], out_ref.shape[0] // CAP)
    table = (first | second).astype(jnp.bfloat16)
    out = jnp.dot(table, rows_ref[...], preferred_element_type=jnp.float32)
    out_ref[...] = out.astype(jnp.bfloat16)


def combine_kernel(routes_ref, gates_ref, back_ref, out_ref):
    copies, capacity, width = back_ref.shape
    copies = copies * capacity // SLOTS
    first, second = slot_table(routes_ref[...], SLOTS // CAP)
    weight = jnp.where(first, gates_ref[0:1, :], 0.0) + jnp.where(second, gates_ref[1:2, :], 0.0)
    high = weight.astype(jnp.bfloat16)
    low = (weight - high.astype(jnp.float32)).astype(jnp.bfloat16)
    back = back_ref[...].reshape(copies * SLOTS, width)
    high, low = jnp.concatenate([high] * copies, axis=0), jnp.concatenate([low] * copies, axis=0)
    dims = (((0,), (0,)), ((), ()))
    out = lax.dot_general(high, back, dims, preferred_element_type=jnp.float32)
    out = out + lax.dot_general(low, back, dims, preferred_element_type=jnp.float32)
    out_ref[...] = out.astype(jnp.bfloat16)


def attend_kernel(lengths_ref, queries_ref, cache_ref, *refs):
    weights, out_ref, copies, sems = refs[:3], refs[3], refs[4:7], refs[7]

    def weight_copy(i):
        return pltpu.make_async_copy(weights[i], copies[i], sems.at[i])

    for i in range(3):
        pl.when(pl.program_id(0) == i)(weight_copy(i).start)

    length = lengths_ref[pl.program_id(0)]
    scores = lax.dot_general(
        queries_ref[0], cache_ref[0], (((0,), (0,)), ((), ())), preferred_element_type=jnp.float32
    )
    visible = lax.broadcasted_iota(jnp.int32, scores.shape, 1) < length
    scores = jnp.where(visible, scores, -1e30)
    top = jnp.max(scores, axis=1, keepdims=True)
    probs = jnp.exp2((scores - top) * (SCORE_SCALE * LOG2_E))
    total = jnp.sum(probs, axis=1, keepdims=True)
    out = lax.dot_general(
        probs.astype(jnp.bfloat16),
        cache_ref[0, :KV, :],
        (((1,), (1,)), ((), ())),
        preferred_element_type=jnp.float32,
    )
    out_ref[0] = (out / total).astype(jnp.bfloat16)

    @pl.when(pl.program_id(0) == pl.num_programs(0) - 1)
    def _():
        for i in range(3):
            weight_copy(i).wait()


def attend(queries, latent_cache, lengths, weights):
    rows, heads, width = queries.shape
    context = latent_cache.shape[1]
    in_hbm = [pltpu.with_memory_space_constraint(w, pltpu.HBM) for w in weights]
    cache = pltpu.with_memory_space_constraint(jnp.swapaxes(latent_cache, 1, 2), pltpu.HBM)
    return pl.pallas_call(
        attend_kernel,
        grid=(rows,),
        out_shape=(
            jax.ShapeDtypeStruct((rows, heads, KV), jnp.bfloat16),
            *[pltpu.VMEM(w.shape, w.dtype) for w in weights],
        ),
        in_specs=[
            pl.BlockSpec(memory_space=pltpu.SMEM),
            pl.BlockSpec((1, width, heads), lambda r: (r, 0, 0)),
            pl.BlockSpec((1, width, context), lambda r: (r, 0, 0)),
            *[pl.BlockSpec(memory_space=pl.ANY)] * 3,
        ],
        out_specs=(
            pl.BlockSpec((1, heads, KV), lambda r: (r, 0, 0)),
            *[pl.BlockSpec(memory_space=pl.ANY)] * 3,
        ),
        scratch_shapes=[pltpu.SemaphoreType.DMA((3,))],
        compiler_params=pltpu.CompilerParams(vmem_limit_bytes=16 * 2**20),
        cost_estimate=SMALL,
    )(lengths, jnp.swapaxes(queries, 1, 2), cache, *in_hbm)


STEPS = 7


def expert_kernel(count, *refs):
    blocks, (gate_ref, up_ref, down_ref, mine_ref, *theirs_refs) = refs[:count], refs[count:]
    rows = jnp.concatenate([b[...] for b in blocks], axis=0)
    gate_act = jnp.dot(rows, gate_ref[0], preferred_element_type=jnp.float32)
    up_act = jnp.dot(rows, up_ref[0], preferred_element_type=jnp.float32)
    hidden = (gate_act / (1.0 + jnp.exp(-gate_act)) * up_act).astype(jnp.bfloat16)
    half = hidden.shape[0] // 2
    depth = down_ref.shape[2] // STEPS
    for step in range(STEPS):
        part = pl.ds(step * depth, depth)
        out = jnp.dot(hidden, down_ref[0, :, part], preferred_element_type=jnp.float32)
        out = out.astype(jnp.bfloat16)
        size = half // len(theirs_refs)
        for i, theirs_ref in enumerate(theirs_refs):
            theirs_ref[:, part] = out[i * size : (i + 1) * size]
        mine_ref[:, part] = out[half:]


def experts_on(theirs, mine, gate_w, up_w, down_w):
    rows, width = mine[0].shape
    hidden = gate_w.shape[2]
    mine_out = pltpu.VMEM((len(mine) * rows, width), jnp.bfloat16)
    parts = max(1, len(mine) * rows // SLOTS)
    theirs_out = pltpu.VMEM((SLOTS, width), jnp.bfloat16)
    total = 2 * len(mine) * rows

    def kernel(*refs):
        expert_kernel(2 * len(mine), *refs)

    return pl.pallas_call(
        kernel,
        out_shape=(mine_out,) + (theirs_out,) * parts,
        in_specs=[VMEM] * (2 * len(mine) + 3),
        out_specs=(VMEM,) * (1 + parts),
        compiler_params=pltpu.CompilerParams(vmem_limit_bytes=16 * 2**20),
        cost_estimate=SMALL,
    )(*theirs, *mine, gate_w, up_w, down_w)


def shift(size, by):
    return [(i, (i + by) % size) for i in range(size)]


def add_up(first, *others):
    total = first.astype(jnp.float32)
    for other in others:
        total = total + other.astype(jnp.float32)
    return total.astype(jnp.bfloat16)


def sum_kernel(near_ref, own_back, below_back, above_back, far_ref, far_back_ref, out_ref):
    slots, width = far_ref.shape
    columns = out_ref.shape[0] * CAP // slots
    me = lax.axis_index("y")

    def put(by, block):
        column = lax.rem(me + (columns - by), columns)
        place = pl.ds(column * (slots // CAP), slots // CAP)
        out_ref[place] = block.reshape(slots // CAP, CAP, width)

    for i, (by, back_ref) in enumerate(((0, own_back), (1, below_back), (3, above_back))):
        put(by, add_up(near_ref[pl.ds(i * slots, slots), :], back_ref[...]))
    put(2, add_up(far_ref[...], far_back_ref[...]))


def body(moe_in, routes, gates, gate_w, up_w, down_w, queries, latent_cache, lengths):
    experts = lax.axis_size("x") * lax.axis_size("z")
    columns = lax.axis_size("y")
    width = moe_in.shape[1]
    slots = experts * CAP
    routes, gates = routes.T, gates.T
    flat = jax.ShapeDtypeStruct((slots, width), jnp.bfloat16)
    outgoing = pl.pallas_call(
        send_kernel,
        out_shape=flat,
        in_specs=[VMEM, VMEM],
        out_specs=VMEM,
        compiler_params=pltpu.CompilerParams(vmem_limit_bytes=4 * 2**20),
    )(*[pltpu.with_memory_space_constraint(a, pltpu.HBM) for a in (routes, moe_in)])
    outgoing = outgoing.reshape(experts, CAP, width)
    own = lax.all_to_all(outgoing, ("x", "z"), split_axis=0, concat_axis=0, tiled=True)
    own = own.reshape(slots, width)
    swap = shift(2, 1)
    near = [lax.ppermute(own, "y", shift(columns, by)) for by in (1, 3)]
    own_theirs = lax.ppermute(own, "core", swap)
    attended, *weights = attend(queries, latent_cache, lengths, (gate_w, up_w, down_w))
    *near, attended = lax.optimization_barrier((*near, attended))
    half = slots // 2
    far = [
        lax.ppermute(near[0][:half], "y", shift(columns, 1)),
        lax.ppermute(near[1][half:], "y", shift(columns, 3)),
    ]
    near_theirs = [lax.ppermute(block, "core", swap) for block in near]
    near_out = experts_on([own_theirs] + near_theirs, [own] + near, *weights)
    near_back = [lax.ppermute(block, "core", swap) for block in near_out[1:]]
    far[0], far[1], near_mine = lax.optimization_barrier((*far, near_out[0]))
    far_theirs = [lax.ppermute(block, "core", swap) for block in far]
    far_out = experts_on(far_theirs, far, *weights)
    far_back = lax.ppermute(far_out[1], "core", swap)
    summed = pl.pallas_call(
        sum_kernel,
        out_shape=jax.ShapeDtypeStruct((columns * experts, CAP, width), jnp.bfloat16),
        in_specs=[VMEM] * 6,
        out_specs=VMEM,
        compiler_params=pltpu.CompilerParams(vmem_limit_bytes=16 * 2**20),
        cost_estimate=SMALL,
    )(near_mine, *near_back, far_out[0], far_back)
    returned = lax.all_to_all(summed, ("y", "x", "z"), split_axis=0, concat_axis=0, tiled=True)
    moe_out = pl.pallas_call(
        combine_kernel,
        out_shape=jax.ShapeDtypeStruct(moe_in.shape, jnp.bfloat16),
        in_specs=[VMEM, VMEM, VMEM],
        out_specs=VMEM,
        compiler_params=pltpu.CompilerParams(vmem_limit_bytes=4 * 2**20),
    )(routes, gates, returned)
    return (moe_out, attended)


def solution(mesh):
    devices = mesh.devices
    split = Mesh(devices.reshape(devices.shape[0] // 2, 2, 4, 4), ("y", "core", "x", "z"))
    attn, exp = ("y", "core"), ("x", "z")
    both = attn + exp
    placed = (
        P(both, None),
        P(both, None),
        P(both, None),
        P(exp, None, attn),
        P(exp, None, attn),
        P(exp, attn, None),
        P(both, None, None),
        P(both, None, None),
        P(both),
    )
    return jax.shard_map(
        body,
        mesh=split,
        in_specs=placed,
        out_specs=(P(both, None), P(both, None, None)),
        check_vma=False,
    )
```

time: 130 us -> 85.9 us (0.66)
  matrix products: 38.5 us -> 0 us
  local copies, waits for them, and re-layouts: 26.8 us -> 1.05 us
  Pallas kernels: 0 us -> 17.1 us
  blocking collectives: 38.2 us -> 52.4 us
  waiting for transfers between devices: 13.1 us -> 5.9 us
  other arithmetic: 6.24 us -> 0 us
  starting transfers between devices: 5.93 us -> 8.57 us
    dot_general x8 -> x0, matrix products: 30 us -> none  [the longest x2 13.7 us: expert_slice(): out = jnp.dot(hidden, down_w, preferred_element_type=jnp.float32)]
    pallas_call x0 -> x6, Pallas kernels: none -> 17.1 us  [the longest x1 9.09 us: attend(): pl.pallas_call(attend_kernel, grid=(rows,), out_shape=(jax.ShapeDtypeStru...]
    reshape x4 -> x2, local copies, waits for them, and re-layouts: 17 us -> 0.35 us  [the longest x1 0.17 us: body(): outgoing = outgoing.reshape(experts, CAP, width)]
    all_to_all x1 -> x2, blocking collectives: 38.2 us -> 52.4 us  [the longest x1 33.8 us: body(): lax.all_to_all(summed, ('y', 'x', 'z'), split_axis=0, concat_axis=0, tile...]
    all_to_all x1 -> x0, waiting for transfers between devices: 10.4 us -> none  [body(): lax.all_to_all(summed, chips, split_axis=0, concat_axis=0, tiled=True)]
    sub x1 -> x0, matrix products: 8.5 us -> none  [attend(): exp_scores = jnp.where(visible, jnp.exp(scores - row_max), 0.0)]
    ppermute x2 -> x13, starting transfers between devices: 0.14 us -> 8.57 us  [the longest x2 3.31 us: body(): near = [lax.ppermute(own, 'y', shift(columns, by)) for by in (1, 3)]]
    convert_element_type x3 -> x0, other arithmetic: 5.84 us -> none  [the longest x1 5.76 us: body(): (part_mine.astype(jnp.float32) + part_back.astype(jnp.float32)).astype(jn...]
  transfers between devices with their start and end apart: 3 -> 13, of which waited for: 2 -> 4; matrix products, arithmetic and copies ran while one was open for 28% -> 0% of each run, Pallas kernels for 0% -> 16%
where the time goes in v3:
time: 85.9 us; the launch traced here: 85.7 us
  blocking collectives  52.4 us (61%)
  Pallas kernels  17.1 us (20%)
  starting transfers between devices  8.57 us (10%)
  waiting for transfers between devices  5.9 us (7%)
  local copies, waits for them, and re-layouts  1.05 us (1%)
    all_to_all x1, blocking collectives, body(): lax.all_to_all(summed, ('y', 'x', 'z'), split_axis=0, concat_axis=0, tile...  33.8 us
    all_to_all x1, blocking collectives, body(): lax.all_to_all(outgoing, ('x', 'z'), split_axis=0, concat_axis=0, tiled=T...  18.6 us
    pallas_call x1, Pallas kernels, attend(): pl.pallas_call(attend_kernel, grid=(rows,), out_shape=(jax.ShapeDtypeStru...  9.09 us
    pallas_call x2, Pallas kernels, experts_on(): pl.pallas_call(kernel, out_shape=(mine_out,) + (theirs_out,) * parts, in_...  4.55 us
    ppermute x1, waiting for transfers between devices, body(): lax.ppermute(near[0][:half], 'y', shift(columns, 1))  3.46 us
    ppermute x2, starting transfers between devices, body(): near = [lax.ppermute(own, 'y', shift(columns, by)) for by in (1, 3)]  3.31 us
    ppermute x1, starting transfers between devices, body(): lax.ppermute(near[1][half:], 'y', shift(columns, 3))  2.8 us
  transfers between devices with their start and end apart: 13, of which 4 were waited for; matrix products, arithmetic and copies ran while one was open for 0% of the time, Pallas kernels for 16%

profile of v3, /device:TPU:0, one launch (start us, length us, event | category | flops | bytes accessed | tf_op | source)
XLA Modules:
  0.0 85.7 jit_solution(167479118963261209)
XLA Ops:
  0.6 1.3 %shard_map.104 = bf16[32,7168]{1,0:T(8,128)(2,1)S(1)} custom-call(s32[2,6]{1,0:T(2,128)} %bitcast.5, bf16[6,7168]{1,0:T(8,128)(2,1)} %rows_ref.1), custom_call_target="tpu_custom_call" | custom-call | tf_op jit(solution)/shard_map/pallas_call | solution.py:189
  2.0 0.2 reshape.10
  2.2 18.6 %all_to_all.10 = bf16[16,2,7168]{2,1,0:T(2,128)(2,1)S(1)} all-to-all(bf16[16,2,7168]{2,1,0:T(2,128)(2,1)S(1)} %reshape.10), channel_id=1, replica_groups=mesh['y'=4,'core'=2,'x'=4,'z'=4] {'x','z'}, dimensions={0} | all-to-all | bytes 917504 | tf_op jit(solution)/shard_map/all_to_all | solution.py:197
  20.7 0.2 reshape.11.refs_3_
  20.9 1.6 %collective-permute-start = (bf16[32,7168]{1,0:T(8,128)(2,1)S(1)}, bf16[32,7168]{1,0:T(8,128)(2,1)S(1)}, u32[]{:S(2)}, u32[]{:S(2)}) collective-permute-start(bf16[32,7168]{1,0:T(8,128)(2,1)S(1)} %reshape.11.refs_3_), channel_id=1, source_target_pairs={{0,32},{32,64},{64,96},{96,0},{1,33},{33,65},{65,97},{97,1},{2,34}... | collective-permute-start | bytes 1376264 | tf_op jit(solution)/shard_map/ppermute | solution.py:200
  22.5 1.7 %collective-permute-start.1 = (bf16[32,7168]{1,0:T(8,128)(2,1)S(1)}, bf16[32,7168]{1,0:T(8,128)(2,1)S(1)}, u32[]{:S(2)}, u32[]{:S(2)}) collective-permute-start(bf16[32,7168]{1,0:T(8,128)(2,1)S(1)} %reshape.11.refs_3_), channel_id=1, source_target_pairs={{0,96},{32,0},{64,32},{96,64},{1,97},{33,1},{65,33},{97,65},{2,98}... | collective-permute-start | bytes 1376264 | tf_op jit(solution)/shard_map/ppermute | solution.py:200
  24.2 0.7 copy-done.3
  24.9 9.1 %shard_map.105 = (bf16[4,128,512]{2,1,0:T(8,128)(2,1)}, bf16[1,7168,256]{2,1,0:T(8,128)(2,1)S(1)}, bf16[1,7168,256]{2,1,0:T(8,128)(2,1)S(1)}, bf16[1,256,7168]{2,1,0:T(8,128)(2,1)S(1)}) custom-call(s32[4]{0:T(128)S(1)} %copy-done.3, bf16[4,576,128]{2,1,0:T(8,128)(2,1)S(1)} %bitcast.4, bf16[4,576,2048]{2,1,0:T(8,128)(2,1)} %bitcast.8, ...), custom_call_target="tpu_custom_call" | custom-call | flops 1000 | bytes 1000 | tf_op jit(solution)/shard_map/pallas_call | solution.py:91
  34.1 0.5 collective-permute-start.5
  34.6 0.1 collective-permute-start.6
  34.7 0.5 collective-permute-start.2
  35.2 2.8 %collective-permute-start.3 = (bf16[16,7168]{1,0:T(8,128)(2,1)S(1)}, bf16[16,7168]{1,0:T(8,128)(2,1)S(1)}, u32[]{:S(2)}, u32[]{:S(2)}) collective-permute-start(bf16[16,7168]{1,0:T(8,128)(2,1)S(1)} %slice.7), channel_id=1, source_target_pairs={{0,96},{32,0},{64,32},{96,64},{1,97},{33,1},{65,33},{97,65},{2,98}... | collective-permute-start | bytes 688136 | tf_op jit(solution)/shard_map/ppermute | solution.py:207
  38.0 2.4 %shard_map.106 = (bf16[96,7168]{1,0:T(8,128)(2,1)S(1)}, bf16[32,7168]{1,0:T(8,128)(2,1)S(1)}, bf16[32,7168]{1,0:T(8,128)(2,1)S(1)}, bf16[32,7168]{1,0:T(8,128)(2,1)S(1)}) custom-call(bf16[32,7168]{1,0:T(8,128)(2,1)S(1)} %collective-permute-done.4.refs_0_, bf16[32,7168]{1,0:T(8,128)(2,1)S(1)} %collective-permute-done.5.refs_1_, ...), custom_call_target="tpu_custom_call" | custom-call | flops 1000 | bytes 1000 | tf_op jit(solution)/shard_map/pallas_call | solution.py:146
  40.5 3.5 %collective-permute-done.2.refs_2_ = bf16[16,7168]{1,0:T(8,128)(2,1)S(1)} collective-permute-done((bf16[16,7168]{1,0:T(8,128)(2,1)S(1)}, bf16[16,7168]{1,0:T(8,128)(2,1)S(1)}, u32[]{:S(2)}, u32[]{:S(2)}) %collective-permute-start.2) | collective-permute-done | bytes 229408 | tf_op jit(solution)/shard_map/ppermute | solution.py:206
  43.9 0.5 collective-permute-start.11
  44.4 0.5 collective-permute-start.8
  45.0 0.5 collective-permute-done.10.refs_0_
  45.4 0.3 collective-permute-done.11.refs_1_
  45.8 2.1 %shard_map.107 = (bf16[32,7168]{1,0:T(8,128)(2,1)S(1)}, bf16[32,7168]{1,0:T(8,128)(2,1)S(1)}) custom-call(bf16[16,7168]{1,0:T(8,128)(2,1)S(1)} %collective-permute-done.10.refs_0_, bf16[16,7168]{1,0:T(8,128)(2,1)S(1)} %collective-permute-done.11.refs_1_, bf16[16,7168]{1,0:T(8,128)(2,1)S(1)} %collective-permute-done.2.refs_2_, ...), custom_call_target="tpu_custom_call" | custom-call | flops 1000 | bytes 1000 | tf_op jit(solution)/shard_map/pallas_call | solution.py:146
  47.9 0.3 collective-permute-start.12
  48.2 1.6 %collective-permute-done.12.far_back_ref = bf16[32,7168]{1,0:T(8,128)(2,1)S(1)} collective-permute-done((bf16[32,7168]{1,0:T(8,128)(2,1)S(1)}, bf16[32,7168]{1,0:T(8,128)(2,1)S(1)}, u32[]{:S(2)}, u32[]{:S(2)}) %collective-permute-start.12) | collective-permute-done | bytes 458784 | tf_op jit(solution)/shard_map/ppermute | solution.py:215
  49.8 0.7 shard_map.108
  50.4 33.8 %all_to_all.11.back_ref = bf16[64,2,7168]{2,1,0:T(2,128)(2,1)S(1)} all-to-all(bf16[64,2,7168]{2,1,0:T(2,128)(2,1)S(1)} %shard_map.108), channel_id=1, replica_groups=mesh['y'=4,'core'=2,'x'=4,'z'=4] {'y','x','z'}, dimensions={0} | all-to-all | bytes 3670016 | tf_op jit(solution)/shard_map/all_to_all | solution.py:224
  84.3 1.4 %shard_map.109 = bf16[6,7168]{1,0:T(8,128)(2,1)} custom-call(s32[2,6]{1,0:T(2,128)S(1)} %bitcast.6, f32[2,6]{1,0:T(2,128)S(1)} %bitcast.7, bf16[64,2,7168]{2,1,0:T(2,128)(2,1)S(1)} %all_to_all.11.back_ref), custom_call_target="tpu_custom_call" | custom-call | tf_op jit(solution)/shard_map/pallas_call | solution.py:225
  (22 shorter events, 0.2 us)
Async XLA Ops:
  0.6 23.6 %copy-start = (bf16[4,128,576]{1,2,0:T(8,128)(2,1)S(1)}, bf16[4,128,576]{1,2,0:T(8,128)(2,1)}, u32[]{:S(2)}) copy-start(bf16[4,128,576]{1,2,0:T(8,128)(2,1)} %param.15) | copy-start | bytes 1769476
  20.9 13.2 %collective-permute-start = (bf16[32,7168]{1,0:T(8,128)(2,1)S(1)}, bf16[32,7168]{1,0:T(8,128)(2,1)S(1)}, u32[]{:S(2)}, u32[]{:S(2)}) collective-permute-start(bf16[32,7168]{1,0:T(8,128)(2,1)S(1)} %reshape.11.refs_3_), channel_id=1, source_target_pairs={{0,32},{32,64},{64,96},{96,0},{1,33},{33,65},{65,97},{97,1},{2,34}... | collective-permute-start | bytes 1376264 | tf_op jit(solution)/shard_map/ppermute | solution.py:200
  22.5 11.5 %collective-permute-start.1 = (bf16[32,7168]{1,0:T(8,128)(2,1)S(1)}, bf16[32,7168]{1,0:T(8,128)(2,1)S(1)}, u32[]{:S(2)}, u32[]{:S(2)}) collective-permute-start(bf16[32,7168]{1,0:T(8,128)(2,1)S(1)} %reshape.11.refs_3_), channel_id=1, source_target_pairs={{0,96},{32,0},{64,32},{96,64},{1,97},{33,1},{65,33},{97,65},{2,98}... | collective-permute-start | bytes 1376264 | tf_op jit(solution)/shard_map/ppermute | solution.py:200
  24.2 0.7 copy-start.3
  34.0 4.1 %collective-permute-start.4 = (bf16[32,7168]{1,0:T(8,128)(2,1)S(1)}, bf16[32,7168]{1,0:T(8,128)(2,1)S(1)}, u32[]{:S(2)}, u32[]{:S(2)}) collective-permute-start(bf16[32,7168]{1,0:T(8,128)(2,1)S(1)} %reshape.11.refs_3_), channel_id=1, source_target_pairs={{0,16},{16,0},{1,17},{17,1},{2,18},{18,2},{3,19},{19,3},{4,20},{20... | collective-permute-start | bytes 1376264 | tf_op jit(solution)/shard_map/ppermute | solution.py:201
  34.1 3.9 %collective-permute-start.5 = (bf16[32,7168]{1,0:T(8,128)(2,1)S(1)}, bf16[32,7168]{1,0:T(8,128)(2,1)S(1)}, u32[]{:S(2)}, u32[]{:S(2)}) collective-permute-start(bf16[32,7168]{1,0:T(8,128)(2,1)S(1)} %collective-permute-done.refs_4_), channel_id=1, source_target_pairs={{0,16},{16,0},{1,17},{17,1},{2,18},{18,2},{3,19},{19,3},{4,20},{20... | collective-permute-start | bytes 1376264 | tf_op jit(solution)/shard_map/ppermute | solution.py:209
  34.6 3.5 %collective-permute-start.6 = (bf16[32,7168]{1,0:T(8,128)(2,1)S(1)}, bf16[32,7168]{1,0:T(8,128)(2,1)S(1)}, u32[]{:S(2)}, u32[]{:S(2)}) collective-permute-start(bf16[32,7168]{1,0:T(8,128)(2,1)S(1)} %collective-permute-done.1.refs_5_), channel_id=1, source_target_pairs={{0,16},{16,0},{1,17},{17,1},{2,18},{18,2},{3,19},{19,3},{4,20},{20... | collective-permute-start | bytes 1376264 | tf_op jit(solution)/shard_map/ppermute | solution.py:209
  34.7 9.2 %collective-permute-start.2 = (bf16[16,7168]{1,0:T(8,128)(2,1)S(1)}, bf16[16,7168]{1,0:T(8,128)(2,1)S(1)}, u32[]{:S(2)}, u32[]{:S(2)}) collective-permute-start(bf16[16,7168]{1,0:T(8,128)(2,1)S(1)} %slice.6), channel_id=1, source_target_pairs={{0,32},{32,64},{64,96},{96,0},{1,33},{33,65},{65,97},{97,1},{2,34}... | collective-permute-start | bytes 688136 | tf_op jit(solution)/shard_map/ppermute | solution.py:206
  35.2 8.7 %collective-permute-start.3 = (bf16[16,7168]{1,0:T(8,128)(2,1)S(1)}, bf16[16,7168]{1,0:T(8,128)(2,1)S(1)}, u32[]{:S(2)}, u32[]{:S(2)}) collective-permute-start(bf16[16,7168]{1,0:T(8,128)(2,1)S(1)} %slice.7), channel_id=1, source_target_pairs={{0,96},{32,0},{64,32},{96,64},{1,97},{33,1},{65,33},{97,65},{2,98}... | collective-permute-start | bytes 688136 | tf_op jit(solution)/shard_map/ppermute | solution.py:207
  43.9 1.5 %collective-permute-start.10 = (bf16[16,7168]{1,0:T(8,128)(2,1)S(1)}, bf16[16,7168]{1,0:T(8,128)(2,1)S(1)}, u32[]{:S(2)}, u32[]{:S(2)}) collective-permute-start(bf16[16,7168]{1,0:T(8,128)(2,1)S(1)} %collective-permute-done.2.refs_2_), channel_id=1, source_target_pairs={{0,16},{16,0},{1,17},{17,1},{2,18},{18,2},{3,19},{19,3},{4,20},{20... | collective-permute-start | bytes 688136 | tf_op jit(solution)/shard_map/ppermute | solution.py:213
  43.9 1.8 %collective-permute-start.11 = (bf16[16,7168]{1,0:T(8,128)(2,1)S(1)}, bf16[16,7168]{1,0:T(8,128)(2,1)S(1)}, u32[]{:S(2)}, u32[]{:S(2)}) collective-permute-start(bf16[16,7168]{1,0:T(8,128)(2,1)S(1)} %collective-permute-done.3.refs_3_), channel_id=1, source_target_pairs={{0,16},{16,0},{1,17},{17,1},{2,18},{18,2},{3,19},{19,3},{4,20},{20... | collective-permute-start | bytes 688136 | tf_op jit(solution)/shard_map/ppermute | solution.py:213
  44.4 3.7 %collective-permute-start.7 = (bf16[32,7168]{1,0:T(8,128)(2,1)S(1)}, bf16[32,7168]{1,0:T(8,128)(2,1)S(1)}, u32[]{:S(2)}, u32[]{:S(2)}) collective-permute-start(bf16[32,7168]{1,0:T(8,128)(2,1)S(1)} %get-tuple-element.26), channel_id=1, source_target_pairs={{0,16},{16,0},{1,17},{17,1},{2,18},{18,2},{3,19},{19,3},{4,20},{20... | collective-permute-start | bytes 1376264 | tf_op jit(solution)/shard_map/ppermute | solution.py:211
  44.4 3.7 %collective-permute-start.8 = (bf16[32,7168]{1,0:T(8,128)(2,1)S(1)}, bf16[32,7168]{1,0:T(8,128)(2,1)S(1)}, u32[]{:S(2)}, u32[]{:S(2)}) collective-permute-start(bf16[32,7168]{1,0:T(8,128)(2,1)S(1)} %get-tuple-element.27), channel_id=1, source_target_pairs={{0,16},{16,0},{1,17},{17,1},{2,18},{18,2},{3,19},{19,3},{4,20},{20... | collective-permute-start | bytes 1376264 | tf_op jit(solution)/shard_map/ppermute | solution.py:211
  45.0 3.2 %collective-permute-start.9 = (bf16[32,7168]{1,0:T(8,128)(2,1)S(1)}, bf16[32,7168]{1,0:T(8,128)(2,1)S(1)}, u32[]{:S(2)}, u32[]{:S(2)}) collective-permute-start(bf16[32,7168]{1,0:T(8,128)(2,1)S(1)} %get-tuple-element.28), channel_id=1, source_target_pairs={{0,16},{16,0},{1,17},{17,1},{2,18},{18,2},{3,19},{19,3},{4,20},{20... | collective-permute-start | bytes 1376264 | tf_op jit(solution)/shard_map/ppermute | solution.py:211
  47.9 1.9 %collective-permute-start.12 = (bf16[32,7168]{1,0:T(8,128)(2,1)S(1)}, bf16[32,7168]{1,0:T(8,128)(2,1)S(1)}, u32[]{:S(2)}, u32[]{:S(2)}) collective-permute-start(bf16[32,7168]{1,0:T(8,128)(2,1)S(1)} %get-tuple-element.32), channel_id=1, source_target_pairs={{0,16},{16,0},{1,17},{17,1},{2,18},{18,2},{3,19},{19,3},{4,20},{20... | collective-permute-start | bytes 1376264 | tf_op jit(solution)/shard_map/ppermute | solution.py:215
  49.8 34.5 %copy-start.1 = (s32[6,2]{0,1:T(2,128)S(1)}, s32[6,2]{0,1:T(2,128)}, u32[]{:S(2)}) copy-start(s32[6,2]{0,1:T(2,128)} %param.10) | copy-start | bytes 148
  49.8 34.5 %copy-start.2 = (f32[6,2]{0,1:T(2,128)S(1)}, f32[6,2]{0,1:T(2,128)}, u32[]{:S(2)}) copy-start(f32[6,2]{0,1:T(2,128)} %param.11) | copy-start | bytes 148

commit v4 on v3

--- a/solution.py
+++ b/solution.py
@@ -1,3 +1,5 @@
+import functools
+
 import jax
 import jax.numpy as jnp
 from jax import lax
@@ -51,64 +53,73 @@
     out_ref[...] = out.astype(jnp.bfloat16)
 
 
-def attend_kernel(lengths_ref, queries_ref, cache_ref, *refs):
-    weights, out_ref, copies, sems = refs[:3], refs[3], refs[4:7], refs[7]
-
-    def weight_copy(i):
-        return pltpu.make_async_copy(weights[i], copies[i], sems.at[i])
-
-    for i in range(3):
-        pl.when(pl.program_id(0) == i)(weight_copy(i).start)
-
-    length = lengths_ref[pl.program_id(0)]
-    scores = lax.dot_general(
-        queries_ref[0], cache_ref[0], (((0,), (0,)), ((), ())), preferred_element_type=jnp.float32
-    )
-    visible = lax.broadcasted_iota(jnp.int32, scores.shape, 1) < length
-    scores = jnp.where(visible, scores, -1e30)
-    top = jnp.max(scores, axis=1, keepdims=True)
-    probs = jnp.exp2((scores - top) * (SCORE_SCALE * LOG2_E))
-    total = jnp.sum(probs, axis=1, keepdims=True)
-    out = lax.dot_general(
-        probs.astype(jnp.bfloat16),
-        cache_ref[0, :KV, :],
-        (((1,), (1,)), ((), ())),
-        preferred_element_type=jnp.float32,
-    )
-    out_ref[0] = (out / total).astype(jnp.bfloat16)
-
-    @pl.when(pl.program_id(0) == pl.num_programs(0) - 1)
-    def _():
-        for i in range(3):
-            weight_copy(i).wait()
-
-
-def attend(queries, latent_cache, lengths, weights):
+PIECES = 4
+
+
+def attend_kernel(lengths_ref, queries_ref, cache_hbm, out_ref, cache_ref, sems):
+    rows, _, context = cache_ref.shape
+    size = context // PIECES
+
+    def for_pieces(row, act):
+        for piece in range(PIECES):
+            part = pl.ds(piece * size, size)
+            copy = pltpu.make_async_copy(
+                cache_hbm.at[row, :, part], cache_ref.at[row, :, part], sems.at[row, piece]
+            )
+            pl.when(lengths_ref[row] > piece * size)(functools.partial(act, copy))
+
+    def attend_to(row, length, most):
+        scores = lax.dot_general(
+            queries_ref[row],
+            cache_ref[row, :, :most],
+            (((0,), (0,)), ((), ())),
+            preferred_element_type=jnp.float32,
+        )
+        visible = lax.broadcasted_iota(jnp.int32, scores.shape, 1) < length
+        scores = jnp.where(visible, scores, -1e30)
+        top = jnp.max(scores, axis=1, keepdims=True)
+        probs = jnp.exp2((scores - top) * (SCORE_SCALE * LOG2_E))
+        total = jnp.sum(probs, axis=1, keepdims=True)
+        out = lax.dot_general(
+            probs.astype(jnp.bfloat16),
+            cache_ref[row, :KV, :most],
+            (((1,), (1,)), ((), ())),
+            preferred_element_type=jnp.float32,
+        )
+        out_ref[row] = (out / total).astype(jnp.bfloat16)
+
+    for row in range(rows):
+        for_pieces(row, lambda copy: copy.start())
+
+    @pl.loop(0, rows)
+    def _(row):
+        length = lengths_ref[row]
+        for_pieces(row, lambda copy: copy.wait())
+        for piece in range(PIECES):
+            here = (length > piece * size) & (length <= (piece + 1) * size)
+            pl.when(here)(functools.partial(attend_to, row, length, (piece + 1) * size))
+
+
+def attend(queries, latent_cache, lengths):
     rows, heads, width = queries.shape
     context = latent_cache.shape[1]
-    in_hbm = [pltpu.with_memory_space_constraint(w, pltpu.HBM) for w in weights]
     cache = pltpu.with_memory_space_constraint(jnp.swapaxes(latent_cache, 1, 2), pltpu.HBM)
     return pl.pallas_call(
         attend_kernel,
-        grid=(rows,),
-        out_shape=(
-            jax.ShapeDtypeStruct((rows, heads, KV), jnp.bfloat16),
-            *[pltpu.VMEM(w.shape, w.dtype) for w in weights],
-        ),
+        out_shape=jax.ShapeDtypeStruct((rows, heads, KV), jnp.bfloat16),
         in_specs=[
             pl.BlockSpec(memory_space=pltpu.SMEM),
-            pl.BlockSpec((1, width, heads), lambda r: (r, 0, 0)),
-            pl.BlockSpec((1, width, context), lambda r: (r, 0, 0)),
-            *[pl.BlockSpec(memory_space=pl.ANY)] * 3,
+            VMEM,
+            pl.BlockSpec(memory_space=pl.ANY),
         ],
-        out_specs=(
-            pl.BlockSpec((1, heads, KV), lambda r: (r, 0, 0)),
-            *[pl.BlockSpec(memory_space=pl.ANY)] * 3,
-        ),
-        scratch_shapes=[pltpu.SemaphoreType.DMA((3,))],
-        compiler_params=pltpu.CompilerParams(vmem_limit_bytes=16 * 2**20),
+        out_specs=VMEM,
+        scratch_shapes=[
+            pltpu.VMEM((rows, width, context), jnp.bfloat16),
+            pltpu.SemaphoreType.DMA((rows, PIECES)),
+        ],
+        compiler_params=pltpu.CompilerParams(vmem_limit_bytes=20 * 2**20),
         cost_estimate=SMALL,
-    )(lengths, jnp.swapaxes(queries, 1, 2), cache, *in_hbm)
+    )(lengths, jnp.swapaxes(queries, 1, 2), cache)
 
 
 STEPS = 7
@@ -133,20 +144,19 @@
 
 
 def experts_on(theirs, mine, gate_w, up_w, down_w):
-    rows, width = mine[0].shape
-    hidden = gate_w.shape[2]
-    mine_out = pltpu.VMEM((len(mine) * rows, width), jnp.bfloat16)
-    parts = max(1, len(mine) * rows // SLOTS)
+    width, hidden = gate_w.shape[1:]
+    rows = sum(block.shape[0] for block in mine)
+    mine_out = pltpu.VMEM((rows, width), jnp.bfloat16)
+    parts = rows // SLOTS
     theirs_out = pltpu.VMEM((SLOTS, width), jnp.bfloat16)
-    total = 2 * len(mine) * rows
 
     def kernel(*refs):
-        expert_kernel(2 * len(mine), *refs)
+        expert_kernel(len(theirs) + len(mine), *refs)
 
     return pl.pallas_call(
         kernel,
         out_shape=(mine_out,) + (theirs_out,) * parts,
-        in_specs=[VMEM] * (2 * len(mine) + 3),
+        in_specs=[VMEM] * (len(theirs) + len(mine) + 3),
         out_specs=(VMEM,) * (1 + parts),
         compiler_params=pltpu.CompilerParams(vmem_limit_bytes=16 * 2**20),
         cost_estimate=SMALL,
@@ -164,7 +174,7 @@
     return total.astype(jnp.bfloat16)
 
 
-def sum_kernel(near_ref, own_back, below_back, above_back, far_ref, far_back_ref, out_ref):
+def sum_kernel(near_ref, own_back, first_back, second_back, far_ref, far_back_ref, out_ref):
     slots, width = far_ref.shape
     columns = out_ref.shape[0] * CAP // slots
     me = lax.axis_index("y")
@@ -174,7 +184,9 @@
         place = pl.ds(column * (slots // CAP), slots // CAP)
         out_ref[place] = block.reshape(slots // CAP, CAP, width)
 
-    for i, (by, back_ref) in enumerate(((0, own_back), (1, below_back), (3, above_back))):
+    core = lax.axis_index("core")
+    backs = ((0, own_back), (1 + 2 * core, first_back), (3 - 2 * core, second_back))
+    for i, (by, back_ref) in enumerate(backs):
         put(by, add_up(near_ref[pl.ds(i * slots, slots), :], back_ref[...]))
     put(2, add_up(far_ref[...], far_back_ref[...]))
 
@@ -197,21 +209,22 @@
     own = lax.all_to_all(outgoing, ("x", "z"), split_axis=0, concat_axis=0, tiled=True)
     own = own.reshape(slots, width)
     swap = shift(2, 1)
-    near = [lax.ppermute(own, "y", shift(columns, by)) for by in (1, 3)]
+    both = ("y", "core")
+    one_way = [(2 * y + c, 2 * ((y + 1 - 2 * c) % columns) + c) for y in range(columns) for c in (0, 1)]
+    other_way = [(there, here) for here, there in one_way]
+    first = lax.ppermute(own, both, one_way)
+    second = lax.ppermute(own, both, other_way)
     own_theirs = lax.ppermute(own, "core", swap)
-    attended, *weights = attend(queries, latent_cache, lengths, (gate_w, up_w, down_w))
-    *near, attended = lax.optimization_barrier((*near, attended))
-    half = slots // 2
-    far = [
-        lax.ppermute(near[0][:half], "y", shift(columns, 1)),
-        lax.ppermute(near[1][half:], "y", shift(columns, 3)),
-    ]
+    attended = attend(queries, latent_cache, lengths)
+    weights = [pltpu.with_memory_space_constraint(w, pltpu.VMEM) for w in (gate_w, up_w, down_w)]
+    first, second, attended = lax.optimization_barrier((first, second, attended))
+    far = lax.ppermute(first, both, one_way)
+    near = [first, second]
     near_theirs = [lax.ppermute(block, "core", swap) for block in near]
     near_out = experts_on([own_theirs] + near_theirs, [own] + near, *weights)
     near_back = [lax.ppermute(block, "core", swap) for block in near_out[1:]]
-    far[0], far[1], near_mine = lax.optimization_barrier((*far, near_out[0]))
-    far_theirs = [lax.ppermute(block, "core", swap) for block in far]
-    far_out = experts_on(far_theirs, far, *weights)
+    far, near_mine = lax.optimization_barrier((far, near_out[0]))
+    far_out = experts_on([lax.ppermute(far, "core", swap)], [far], *weights)
     far_back = lax.ppermute(far_out[1], "core", swap)
     summed = pl.pallas_call(
         sum_kernel,

time: 85.9 us -> 84.5 us (0.984)
  starting transfers between devices: 8.57 us -> 5.83 us
  waiting for transfers between devices: 5.9 us -> 8.12 us
  local copies, waits for them, and re-layouts: 1.05 us -> 3.06 us
  Pallas kernels: 17.1 us -> 15.5 us
  blocking collectives: 52.4 us -> 51.1 us
    ppermute x6 -> x4, starting transfers between devices: 7.12 us -> 4.01 us  [the longest x1 3.08 us: body(): second = lax.ppermute(own, both, other_way)]
    unnamed x8 -> x14, local copies, waits for them, and re-layouts: 0.67 us -> 2.71 us
    pallas_call x1, Pallas kernels: 9.09 us -> 7.56 us  [attend(): pl.pallas_call(attend_kernel, out_shape=jax.ShapeDtypeStruct((rows, heads...]
    all_to_all x1, blocking collectives: 33.8 us -> 32.5 us  [body(): lax.all_to_all(summed, ('y', 'x', 'z'), split_axis=0, concat_axis=0, tile...]
    ppermute x6 -> x4, waiting for transfers between devices: 4.26 us -> 5.4 us  [the longest x1 3.25 us: body(): far = lax.ppermute(first, both, one_way)]
    ppermute x2, waiting for transfers between devices: 0.01 us -> 1.04 us  [body(): near_theirs = [lax.ppermute(block, 'core', swap) for block in near]]
  transfers between devices with their start and end apart: 13 -> 11, of which waited for: 4 -> 7; matrix products, arithmetic and copies ran while one was open for 0% -> 0% of each run, Pallas kernels for 16% -> 14%
where the time goes in v4:
time: 84.5 us; the launch traced here: 84.3 us
  blocking collectives  51.1 us (60%)
  Pallas kernels  15.5 us (18%)
  waiting for transfers between devices  8.12 us (10%)
  starting transfers between devices  5.83 us (7%)
  local copies, waits for them, and re-layouts  3.06 us (4%)
    all_to_all x1, blocking collectives, body(): lax.all_to_all(summed, ('y', 'x', 'z'), split_axis=0, concat_axis=0, tile...  32.5 us
    all_to_all x1, blocking collectives, body(): lax.all_to_all(outgoing, ('x', 'z'), split_axis=0, concat_axis=0, tiled=T...  18.6 us
    pallas_call x1, Pallas kernels, attend(): pl.pallas_call(attend_kernel, out_shape=jax.ShapeDtypeStruct((rows, heads...  7.56 us
    pallas_call x2, Pallas kernels, experts_on(): pl.pallas_call(kernel, out_shape=(mine_out,) + (theirs_out,) * parts, in_...  4.53 us
    ppermute x1, waiting for transfers between devices, body(): far = lax.ppermute(first, both, one_way)  3.25 us
    ppermute x1, starting transfers between devices, body(): second = lax.ppermute(own, both, other_way)  3.08 us
    unnamed x14, local copies, waits for them, and re-layouts  2.71 us
  transfers between devices with their start and end apart: 11, of which 7 were waited for; matrix products, arithmetic and copies ran while one was open for 0% of the time, Pallas kernels for 14%

profile of v4, /device:TPU:0, one launch (start us, length us, event | category | flops | bytes accessed | tf_op | source)
XLA Modules:
  0.0 84.3 jit_solution(16617871225679589143)
XLA Ops:
  0.6 1.3 %shard_map.104 = bf16[32,7168]{1,0:T(8,128)(2,1)S(1)} custom-call(s32[2,6]{1,0:T(2,128)} %bitcast.5, bf16[6,7168]{1,0:T(8,128)(2,1)} %rows_ref.1), custom_call_target="tpu_custom_call" | custom-call | tf_op jit(solution)/shard_map/pallas_call | solution.py:201
  2.0 0.2 reshape.10
  2.2 18.6 %all_to_all.10 = bf16[16,2,7168]{2,1,0:T(2,128)(2,1)S(1)} all-to-all(bf16[16,2,7168]{2,1,0:T(2,128)(2,1)S(1)} %reshape.10), channel_id=1, replica_groups=mesh['y'=4,'core'=2,'x'=4,'z'=4] {'x','z'}, dimensions={0} | all-to-all | bytes 917504 | tf_op jit(solution)/shard_map/all_to_all | solution.py:209
  20.9 3.1 %collective-permute-start.1 = (bf16[32,7168]{1,0:T(8,128)(2,1)S(1)}, bf16[32,7168]{1,0:T(8,128)(2,1)S(1)}, u32[]{:S(2)}, u32[]{:S(2)}) collective-permute-start(bf16[32,7168]{1,0:T(8,128)(2,1)S(1)} %reshape.11.refs_3_), channel_id=1, source_target_pairs={{32,0},{112,16},{64,32},{16,48},{96,64},{48,80},{0,96},{80,112},{3... | collective-permute-start | bytes 1376264 | tf_op jit(solution)/shard_map/ppermute | solution.py:216
  24.0 0.7 copy-done.6
  24.7 7.6 %shard_map.105 = bf16[4,128,512]{2,1,0:T(8,128)(2,1)} custom-call(s32[4]{0:T(128)S(1)} %copy-done.6, bf16[4,576,128]{2,1,0:T(8,128)(2,1)S(1)} %bitcast.4, bf16[4,576,2048]{2,1,0:T(8,128)(2,1)} %bitcast.8), custom_call_target="tpu_custom_call" | custom-call | flops 1000 | bytes 1000 | tf_op jit(solution)/shard_map/pallas_call | solution.py:107
  32.3 0.7 collective-permute-done.1.refs_5_
  33.0 0.7 collective-permute-done.refs_4_
  33.7 0.5 collective-permute-start.4
  34.2 0.9 %collective-permute-start.2 = (bf16[32,7168]{1,0:T(8,128)(2,1)S(1)}, bf16[32,7168]{1,0:T(8,128)(2,1)S(1)}, u32[]{:S(2)}, u32[]{:S(2)}) collective-permute-start(bf16[32,7168]{1,0:T(8,128)(2,1)S(1)} %collective-permute-done.refs_4_), channel_id=1, source_target_pairs={{0,32},{16,112},{32,64},{48,16},{64,96},{80,48},{96,0},{112,80},{1... | collective-permute-start | bytes 1376264 | tf_op jit(solution)/shard_map/ppermute | solution.py:221
  35.1 0.4 collective-permute-done.5.refs_2_
  35.5 0.7 collective-permute-done.4.refs_1_
  36.2 2.0 %copy-done.2 = bf16[1,256,7168]{2,1,0:T(8,128)(2,1)S(1)} copy-done((bf16[1,256,7168]{2,1,0:T(8,128)(2,1)S(1)}, bf16[1,256,7168]{2,1,0:T(8,128)(2,1)}, u32[]{:S(2)}) %copy-start.2) | copy-done | bytes 3670040
  38.2 2.4 %shard_map.106 = (bf16[96,7168]{1,0:T(8,128)(2,1)S(1)}, bf16[32,7168]{1,0:T(8,128)(2,1)S(1)}, bf16[32,7168]{1,0:T(8,128)(2,1)S(1)}, bf16[32,7168]{1,0:T(8,128)(2,1)S(1)}) custom-call(bf16[32,7168]{1,0:T(8,128)(2,1)S(1)} %collective-permute-done.3.refs_0_, bf16[32,7168]{1,0:T(8,128)(2,1)S(1)} %collective-permute-done.4.refs_1_, ...), custom_call_target="tpu_custom_call" | custom-call | flops 1000 | bytes 1000 | tf_op jit(solution)/shard_map/pallas_call | solution.py:156
  40.6 3.2 %collective-permute-done.2.refs_1_ = bf16[32,7168]{1,0:T(8,128)(2,1)S(1)} collective-permute-done((bf16[32,7168]{1,0:T(8,128)(2,1)S(1)}, bf16[32,7168]{1,0:T(8,128)(2,1)S(1)}, u32[]{:S(2)}, u32[]{:S(2)}) %collective-permute-start.2) | collective-permute-done | bytes 458784 | tf_op jit(solution)/shard_map/ppermute | solution.py:221
  43.9 0.5 collective-permute-start.6
  44.4 0.5 collective-permute-start.8
  44.9 0.8 collective-permute-done.9.refs_0_
  45.7 2.1 %shard_map.107 = (bf16[32,7168]{1,0:T(8,128)(2,1)S(1)}, bf16[32,7168]{1,0:T(8,128)(2,1)S(1)}) custom-call(bf16[32,7168]{1,0:T(8,128)(2,1)S(1)} %collective-permute-done.9.refs_0_, bf16[32,7168]{1,0:T(8,128)(2,1)S(1)} %collective-permute-done.2.refs_1_, bf16[1,7168,256]{2,1,0:T(8,128)(2,1)S(1)} %copy-done, bf16[1,7168,256]{2,1,0:T(8,128)(2,1)S(1)} %copy-done.1, ...), custom_call_target="tpu_custom_call" | custom-call | flops 1000 | bytes 1000 | tf_op jit(solution)/shard_map/pallas_call | solution.py:156
  47.8 0.2 collective-permute-start.10
  48.0 1.7 %collective-permute-done.10.far_back_ref = bf16[32,7168]{1,0:T(8,128)(2,1)S(1)} collective-permute-done((bf16[32,7168]{1,0:T(8,128)(2,1)S(1)}, bf16[32,7168]{1,0:T(8,128)(2,1)S(1)}, u32[]{:S(2)}, u32[]{:S(2)}) %collective-permute-start.10) | collective-permute-done | bytes 458784 | tf_op jit(solution)/shard_map/ppermute | solution.py:228
  49.7 0.7 shard_map.108
  50.4 32.5 %all_to_all.11.back_ref = bf16[64,2,7168]{2,1,0:T(2,128)(2,1)S(1)} all-to-all(bf16[64,2,7168]{2,1,0:T(2,128)(2,1)S(1)} %shard_map.108), channel_id=1, replica_groups=mesh['y'=4,'core'=2,'x'=4,'z'=4] {'y','x','z'}, dimensions={0} | all-to-all | bytes 3670016 | tf_op jit(solution)/shard_map/all_to_all | solution.py:237
  82.9 1.4 %shard_map.109 = bf16[6,7168]{1,0:T(8,128)(2,1)} custom-call(s32[2,6]{1,0:T(2,128)S(1)} %bitcast.6, f32[2,6]{1,0:T(2,128)S(1)} %bitcast.7, bf16[64,2,7168]{2,1,0:T(2,128)(2,1)S(1)} %all_to_all.11.back_ref), custom_call_target="tpu_custom_call" | custom-call | tf_op jit(solution)/shard_map/pallas_call | solution.py:238
  (22 shorter events, 0.3 us)
Async XLA Ops:
  0.6 23.4 %copy-start.3 = (bf16[4,128,576]{1,2,0:T(8,128)(2,1)S(1)}, bf16[4,128,576]{1,2,0:T(8,128)(2,1)}, u32[]{:S(2)}) copy-start(bf16[4,128,576]{1,2,0:T(8,128)(2,1)} %param.15) | copy-start | bytes 1769476
  20.9 12.1 %collective-permute-start.1 = (bf16[32,7168]{1,0:T(8,128)(2,1)S(1)}, bf16[32,7168]{1,0:T(8,128)(2,1)S(1)}, u32[]{:S(2)}, u32[]{:S(2)}) collective-permute-start(bf16[32,7168]{1,0:T(8,128)(2,1)S(1)} %reshape.11.refs_3_), channel_id=1, source_target_pairs={{32,0},{112,16},{64,32},{16,48},{96,64},{48,80},{0,96},{80,112},{3... | collective-permute-start | bytes 1376264 | tf_op jit(solution)/shard_map/ppermute | solution.py:216
  24.0 9.7 %collective-permute-start = (bf16[32,7168]{1,0:T(8,128)(2,1)S(1)}, bf16[32,7168]{1,0:T(8,128)(2,1)S(1)}, u32[]{:S(2)}, u32[]{:S(2)}) collective-permute-start(bf16[32,7168]{1,0:T(8,128)(2,1)S(1)} %reshape.11.refs_3_), channel_id=1, source_target_pairs={{0,32},{16,112},{32,64},{48,16},{64,96},{80,48},{96,0},{112,80},{1... | collective-permute-start | bytes 1376264 | tf_op jit(solution)/shard_map/ppermute | solution.py:215
  24.0 0.7 copy-start.6
  24.6 11.5 %copy-start = (bf16[1,7168,256]{2,1,0:T(8,128)(2,1)S(1)}, bf16[1,7168,256]{2,1,0:T(8,128)(2,1)}, u32[]{:S(2)}) copy-start(bf16[1,7168,256]{2,1,0:T(8,128)(2,1)} %refs_2_.1) | copy-start | bytes 11010052
  24.7 11.5 %copy-start.1 = (bf16[1,7168,256]{2,1,0:T(8,128)(2,1)S(1)}, bf16[1,7168,256]{2,1,0:T(8,128)(2,1)}, u32[]{:S(2)}) copy-start(bf16[1,7168,256]{2,1,0:T(8,128)(2,1)} %refs_3_.1) | copy-start | bytes 11010052
  32.2 2.9 %collective-permute-start.3 = (bf16[32,7168]{1,0:T(8,128)(2,1)S(1)}, bf16[32,7168]{1,0:T(8,128)(2,1)S(1)}, u32[]{:S(2)}, u32[]{:S(2)}) collective-permute-start(bf16[32,7168]{1,0:T(8,128)(2,1)S(1)} %reshape.11.refs_3_), channel_id=1, source_target_pairs={{0,16},{16,0},{1,17},{17,1},{2,18},{18,2},{3,19},{19,3},{4,20},{20... | collective-permute-start | bytes 1376264 | tf_op jit(solution)/shard_map/ppermute | solution.py:217
  33.7 1.8 %collective-permute-start.5 = (bf16[32,7168]{1,0:T(8,128)(2,1)S(1)}, bf16[32,7168]{1,0:T(8,128)(2,1)S(1)}, u32[]{:S(2)}, u32[]{:S(2)}) collective-permute-start(bf16[32,7168]{1,0:T(8,128)(2,1)S(1)} %collective-permute-done.1.refs_5_), channel_id=1, source_target_pairs={{0,16},{16,0},{1,17},{17,1},{2,18},{18,2},{3,19},{19,3},{4,20},{20... | collective-permute-start | bytes 1376264 | tf_op jit(solution)/shard_map/ppermute | solution.py:223
  33.7 2.5 %collective-permute-start.4 = (bf16[32,7168]{1,0:T(8,128)(2,1)S(1)}, bf16[32,7168]{1,0:T(8,128)(2,1)S(1)}, u32[]{:S(2)}, u32[]{:S(2)}) collective-permute-start(bf16[32,7168]{1,0:T(8,128)(2,1)S(1)} %collective-permute-done.refs_4_), channel_id=1, source_target_pairs={{0,16},{16,0},{1,17},{17,1},{2,18},{18,2},{3,19},{19,3},{4,20},{20... | collective-permute-start | bytes 1376264 | tf_op jit(solution)/shard_map/ppermute | solution.py:223
  34.2 9.7 %collective-permute-start.2 = (bf16[32,7168]{1,0:T(8,128)(2,1)S(1)}, bf16[32,7168]{1,0:T(8,128)(2,1)S(1)}, u32[]{:S(2)}, u32[]{:S(2)}) collective-permute-start(bf16[32,7168]{1,0:T(8,128)(2,1)S(1)} %collective-permute-done.refs_4_), channel_id=1, source_target_pairs={{0,32},{16,112},{32,64},{48,16},{64,96},{80,48},{96,0},{112,80},{1... | collective-permute-start | bytes 1376264 | tf_op jit(solution)/shard_map/ppermute | solution.py:221
  36.2 2.0 %copy-start.2 = (bf16[1,256,7168]{2,1,0:T(8,128)(2,1)S(1)}, bf16[1,256,7168]{2,1,0:T(8,128)(2,1)}, u32[]{:S(2)}) copy-start(bf16[1,256,7168]{2,1,0:T(8,128)(2,1)} %refs_4_.1) | copy-start | bytes 11010052
  43.9 1.8 %collective-permute-start.9 = (bf16[32,7168]{1,0:T(8,128)(2,1)S(1)}, bf16[32,7168]{1,0:T(8,128)(2,1)S(1)}, u32[]{:S(2)}, u32[]{:S(2)}) collective-permute-start(bf16[32,7168]{1,0:T(8,128)(2,1)S(1)} %collective-permute-done.2.refs_1_), channel_id=1, source_target_pairs={{0,16},{16,0},{1,17},{17,1},{2,18},{18,2},{3,19},{19,3},{4,20},{20... | collective-permute-start | bytes 1376264 | tf_op jit(solution)/shard_map/ppermute | solution.py:227
  43.9 4.1 %collective-permute-start.6 = (bf16[32,7168]{1,0:T(8,128)(2,1)S(1)}, bf16[32,7168]{1,0:T(8,128)(2,1)S(1)}, u32[]{:S(2)}, u32[]{:S(2)}) collective-permute-start(bf16[32,7168]{1,0:T(8,128)(2,1)S(1)} %get-tuple-element.17), channel_id=1, source_target_pairs={{0,16},{16,0},{1,17},{17,1},{2,18},{18,2},{3,19},{19,3},{4,20},{20... | collective-permute-start | bytes 1376264 | tf_op jit(solution)/shard_map/ppermute | solution.py:225
  44.4 3.6 %collective-permute-start.7 = (bf16[32,7168]{1,0:T(8,128)(2,1)S(1)}, bf16[32,7168]{1,0:T(8,128)(2,1)S(1)}, u32[]{:S(2)}, u32[]{:S(2)}) collective-permute-start(bf16[32,7168]{1,0:T(8,128)(2,1)S(1)} %get-tuple-element.18), channel_id=1, source_target_pairs={{0,16},{16,0},{1,17},{17,1},{2,18},{18,2},{3,19},{19,3},{4,20},{20... | collective-permute-start | bytes 1376264 | tf_op jit(solution)/shard_map/ppermute | solution.py:225
  44.4 3.6 %collective-permute-start.8 = (bf16[32,7168]{1,0:T(8,128)(2,1)S(1)}, bf16[32,7168]{1,0:T(8,128)(2,1)S(1)}, u32[]{:S(2)}, u32[]{:S(2)}) collective-permute-start(bf16[32,7168]{1,0:T(8,128)(2,1)S(1)} %get-tuple-element.19), channel_id=1, source_target_pairs={{0,16},{16,0},{1,17},{17,1},{2,18},{18,2},{3,19},{19,3},{4,20},{20... | collective-permute-start | bytes 1376264 | tf_op jit(solution)/shard_map/ppermute | solution.py:225
  47.8 1.9 %collective-permute-start.10 = (bf16[32,7168]{1,0:T(8,128)(2,1)S(1)}, bf16[32,7168]{1,0:T(8,128)(2,1)S(1)}, u32[]{:S(2)}, u32[]{:S(2)}) collective-permute-start(bf16[32,7168]{1,0:T(8,128)(2,1)S(1)} %get-tuple-element.22), channel_id=1, source_target_pairs={{0,16},{16,0},{1,17},{17,1},{2,18},{18,2},{3,19},{19,3},{4,20},{20... | collective-permute-start | bytes 1376264 | tf_op jit(solution)/shard_map/ppermute | solution.py:228
  49.7 33.2 %copy-start.4 = (s32[6,2]{0,1:T(2,128)S(1)}, s32[6,2]{0,1:T(2,128)}, u32[]{:S(2)}) copy-start(s32[6,2]{0,1:T(2,128)} %param.10) | copy-start | bytes 148
  49.7 33.2 %copy-start.5 = (f32[6,2]{0,1:T(2,128)S(1)}, f32[6,2]{0,1:T(2,128)}, u32[]{:S(2)}) copy-start(f32[6,2]{0,1:T(2,128)} %param.11) | copy-start | bytes 148

commit v5 on v4

--- a/solution.py
+++ b/solution.py
@@ -43,14 +43,20 @@
     copies = copies * capacity // SLOTS
     first, second = slot_table(routes_ref[...], SLOTS // CAP)
     weight = jnp.where(first, gates_ref[0:1, :], 0.0) + jnp.where(second, gates_ref[1:2, :], 0.0)
+    rows = weight.shape[1]
+    weight = jnp.concatenate([weight, jnp.zeros((SLOTS, 8 - rows % 8), jnp.float32)], axis=1)
     high = weight.astype(jnp.bfloat16)
     low = (weight - high.astype(jnp.float32)).astype(jnp.bfloat16)
-    back = back_ref[...].reshape(copies * SLOTS, width)
-    high, low = jnp.concatenate([high] * copies, axis=0), jnp.concatenate([low] * copies, axis=0)
-    dims = (((0,), (0,)), ((), ()))
-    out = lax.dot_general(high, back, dims, preferred_element_type=jnp.float32)
-    out = out + lax.dot_general(low, back, dims, preferred_element_type=jnp.float32)
-    out_ref[...] = out.astype(jnp.bfloat16)
+    parts = jnp.concatenate([jnp.concatenate([high, low], axis=1)] * copies, axis=0)
+    size = width // STEPS
+    for step in range(STEPS):
+        part = pl.ds(step * size, size)
+        back = back_ref[:, :, part].reshape(copies * SLOTS, size)
+        out = lax.dot_general(
+            parts, back, (((0,), (0,)), ((), ())), preferred_element_type=jnp.float32
+        )
+        out = out[: weight.shape[1]] + out[weight.shape[1] :]
+        out_ref[:, part] = out[:rows].astype(jnp.bfloat16)
 
 
 PIECES = 4
@@ -220,7 +226,10 @@
     first, second, attended = lax.optimization_barrier((first, second, attended))
     far = lax.ppermute(first, both, one_way)
     near = [first, second]
-    near_theirs = [lax.ppermute(block, "core", swap) for block in near]
+    half = slots // 2
+    near_theirs = [
+        lax.ppermute(block[i : i + half], "core", swap) for block in near for i in (0, half)
+    ]
     near_out = experts_on([own_theirs] + near_theirs, [own] + near, *weights)
     near_back = [lax.ppermute(block, "core", swap) for block in near_out[1:]]
     far, near_mine = lax.optimization_barrier((far, near_out[0]))
@@ -241,7 +250,7 @@
         in_specs=[VMEM, VMEM, VMEM],
         out_specs=VMEM,
         compiler_params=pltpu.CompilerParams(vmem_limit_bytes=4 * 2**20),
-    )(routes, gates, returned)
+    )(*[pltpu.with_memory_space_constraint(a, pltpu.VMEM) for a in (routes, gates)], returned)
     return (moe_out, attended)
 
 

time: 84.5 us -> 84 us (level)
  local copies, waits for them, and re-layouts: 3.06 us -> 1.09 us
  Pallas kernels: 15.5 us -> 16.9 us
  starting transfers between devices: 5.83 us -> 6.82 us
    unnamed x14, local copies, waits for them, and re-layouts: 2.71 us -> 0.68 us
    pallas_call x1, Pallas kernels: 7.56 us -> 9.09 us  [attend(): pl.pallas_call(attend_kernel, out_shape=jax.ShapeDtypeStruct((rows, heads...]
    ppermute x2 -> x4, starting transfers between devices: 0.51 us -> 1.63 us  [body(): lax.ppermute(block[i:i + half], 'core', swap)]
  transfers between devices with their start and end apart: 11 -> 13, of which waited for: 7 -> 7; matrix products, arithmetic and copies ran while one was open for 0% -> 0% of each run, Pallas kernels for 14% -> 16%
where the time goes in v5:
time: 84 us; the launch traced here: 83.5 us
  blocking collectives  50.7 us (60%)
  Pallas kernels  16.9 us (20%)
  waiting for transfers between devices  7.29 us (9%)
  starting transfers between devices  6.82 us (8%)
  local copies, waits for them, and re-layouts  1.09 us (1%)
    all_to_all x1, blocking collectives, body(): lax.all_to_all(summed, ('y', 'x', 'z'), split_axis=0, concat_axis=0, tile...  32.1 us
    all_to_all x1, blocking collectives, body(): lax.all_to_all(outgoing, ('x', 'z'), split_axis=0, concat_axis=0, tiled=T...  18.6 us
    pallas_call x1, Pallas kernels, attend(): pl.pallas_call(attend_kernel, out_shape=jax.ShapeDtypeStruct((rows, heads...  9.09 us
    pallas_call x2, Pallas kernels, experts_on(): pl.pallas_call(kernel, out_shape=(mine_out,) + (theirs_out,) * parts, in_...  4.58 us
    ppermute x1, waiting for transfers between devices, body(): far = lax.ppermute(first, both, one_way)  3.27 us
    ppermute x1, starting transfers between devices, body(): second = lax.ppermute(own, both, other_way)  3.08 us
  transfers between devices with their start and end apart: 13, of which 7 were waited for; matrix products, arithmetic and copies ran while one was open for 0% of the time, Pallas kernels for 16%

profile of v5, /device:TPU:0, one launch (start us, length us, event | category | flops | bytes accessed | tf_op | source)
XLA Modules:
  0.0 83.5 jit_solution(2519242726386974947)
XLA Ops:
  0.6 1.3 %shard_map.104 = bf16[32,7168]{1,0:T(8,128)(2,1)S(1)} custom-call(s32[2,6]{1,0:T(2,128)} %bitcast.5, bf16[6,7168]{1,0:T(8,128)(2,1)} %rows_ref.1), custom_call_target="tpu_custom_call" | custom-call | tf_op jit(solution)/shard_map/pallas_call | solution.py:207
  2.0 0.2 reshape.10
  2.2 18.6 %all_to_all.10 = bf16[16,2,7168]{2,1,0:T(2,128)(2,1)S(1)} all-to-all(bf16[16,2,7168]{2,1,0:T(2,128)(2,1)S(1)} %reshape.10), channel_id=1, replica_groups=mesh['y'=4,'core'=2,'x'=4,'z'=4] {'x','z'}, dimensions={0} | all-to-all | bytes 917504 | tf_op jit(solution)/shard_map/all_to_all | solution.py:215
  20.9 3.1 %collective-permute-start.1 = (bf16[32,7168]{1,0:T(8,128)(2,1)S(1)}, bf16[32,7168]{1,0:T(8,128)(2,1)S(1)}, u32[]{:S(2)}, u32[]{:S(2)}) collective-permute-start(bf16[32,7168]{1,0:T(8,128)(2,1)S(1)} %reshape.11.refs_5_), channel_id=1, source_target_pairs={{32,0},{112,16},{64,32},{16,48},{96,64},{48,80},{0,96},{80,112},{3... | collective-permute-start | bytes 1376264 | tf_op jit(solution)/shard_map/ppermute | solution.py:222
  24.0 0.7 copy-done.6
  24.7 9.1 %shard_map.105 = bf16[4,128,512]{2,1,0:T(8,128)(2,1)} custom-call(s32[4]{0:T(128)S(1)} %copy-done.6, bf16[4,576,128]{2,1,0:T(8,128)(2,1)S(1)} %bitcast.4, bf16[4,576,2048]{2,1,0:T(8,128)(2,1)} %bitcast.8), custom_call_target="tpu_custom_call" | custom-call | flops 1000 | bytes 1000 | tf_op jit(solution)/shard_map/pallas_call | solution.py:113
  33.9 0.8 collective-permute-start.2
  34.7 1.0 %collective-permute-start.7 = (bf16[16,7168]{1,0:T(8,128)(2,1)S(1)}, bf16[16,7168]{1,0:T(8,128)(2,1)S(1)}, u32[]{:S(2)}, u32[]{:S(2)}) collective-permute-start(bf16[16,7168]{1,0:T(8,128)(2,1)S(1)} %get-tuple-element.24), channel_id=1, source_target_pairs={{0,16},{16,0},{1,17},{17,1},{2,18},{18,2},{3,19},{19,3},{4,20},{20... | collective-permute-start | bytes 688136 | tf_op jit(solution)/shard_map/ppermute | solution.py:231
  35.9 0.4 collective-permute-start.5
  36.4 0.5 collective-permute-done.7.refs_4_
  36.9 0.4 collective-permute-done.6.refs_3_
  37.2 0.3 collective-permute-done.5.refs_2_
  37.6 0.3 collective-permute-done.4.refs_1_
  37.9 2.5 %shard_map.106 = (bf16[96,7168]{1,0:T(8,128)(2,1)S(1)}, bf16[32,7168]{1,0:T(8,128)(2,1)S(1)}, bf16[32,7168]{1,0:T(8,128)(2,1)S(1)}, bf16[32,7168]{1,0:T(8,128)(2,1)S(1)}) custom-call(bf16[32,7168]{1,0:T(8,128)(2,1)S(1)} %collective-permute-done.3.refs_0_, bf16[16,7168]{1,0:T(8,128)(2,1)S(1)} %collective-permute-done.4.refs_1_, ...), custom_call_target="tpu_custom_call" | custom-call | flops 1000 | bytes 1000 | tf_op jit(solution)/shard_map/pallas_call | solution.py:162
  40.4 3.3 %collective-permute-done.2.refs_1_ = bf16[32,7168]{1,0:T(8,128)(2,1)S(1)} collective-permute-done((bf16[32,7168]{1,0:T(8,128)(2,1)S(1)}, bf16[32,7168]{1,0:T(8,128)(2,1)S(1)}, u32[]{:S(2)}, u32[]{:S(2)}) %collective-permute-start.2) | collective-permute-done | bytes 458784 | tf_op jit(solution)/shard_map/ppermute | solution.py:227
  43.7 0.5 collective-permute-start.8
  44.2 0.5 collective-permute-start.10
  44.7 0.8 collective-permute-done.11.refs_0_
  45.5 2.1 %shard_map.107 = (bf16[32,7168]{1,0:T(8,128)(2,1)S(1)}, bf16[32,7168]{1,0:T(8,128)(2,1)S(1)}) custom-call(bf16[32,7168]{1,0:T(8,128)(2,1)S(1)} %collective-permute-done.11.refs_0_, bf16[32,7168]{1,0:T(8,128)(2,1)S(1)} %collective-permute-done.2.refs_1_, bf16[1,7168,256]{2,1,0:T(8,128)(2,1)S(1)} %copy-done, bf16[1,7168,256]{2,1,0:T(8,128)(2,1)S(1)} %copy-done.1, ...), custom_call_target="tpu_custom_call" | custom-call | flops 1000 | bytes 1000 | tf_op jit(solution)/shard_map/pallas_call | solution.py:162
  47.6 0.2 collective-permute-start.12
  47.8 1.7 %collective-permute-done.12.far_back_ref = bf16[32,7168]{1,0:T(8,128)(2,1)S(1)} collective-permute-done((bf16[32,7168]{1,0:T(8,128)(2,1)S(1)}, bf16[32,7168]{1,0:T(8,128)(2,1)S(1)}, u32[]{:S(2)}, u32[]{:S(2)}) %collective-permute-start.12) | collective-permute-done | bytes 458784 | tf_op jit(solution)/shard_map/ppermute | solution.py:237
  49.5 0.7 shard_map.108
  50.2 32.1 %all_to_all.11.back_ref = bf16[64,2,7168]{2,1,0:T(2,128)(2,1)S(1)} all-to-all(bf16[64,2,7168]{2,1,0:T(2,128)(2,1)S(1)} %shard_map.108), channel_id=1, replica_groups=mesh['y'=4,'core'=2,'x'=4,'z'=4] {'y','x','z'}, dimensions={0} | all-to-all | bytes 3670016 | tf_op jit(solution)/shard_map/all_to_all | solution.py:246
  82.3 1.3 %shard_map.109 = bf16[6,7168]{1,0:T(8,128)(2,1)} custom-call(s32[2,6]{1,0:T(2,128)S(1)} %bitcast.6, f32[2,6]{1,0:T(2,128)S(1)} %bitcast.7, bf16[64,2,7168]{2,1,0:T(2,128)(2,1)S(1)} %all_to_all.11.back_ref), custom_call_target="tpu_custom_call" | custom-call | tf_op jit(solution)/shard_map/pallas_call | solution.py:247
  (28 shorter events, 0.6 us)
Async XLA Ops:
  0.6 23.4 %copy-start.3 = (bf16[4,128,576]{1,2,0:T(8,128)(2,1)S(1)}, bf16[4,128,576]{1,2,0:T(8,128)(2,1)}, u32[]{:S(2)}) copy-start(bf16[4,128,576]{1,2,0:T(8,128)(2,1)} %param.15) | copy-start | bytes 1769476
  20.9 12.9 %collective-permute-start.1 = (bf16[32,7168]{1,0:T(8,128)(2,1)S(1)}, bf16[32,7168]{1,0:T(8,128)(2,1)S(1)}, u32[]{:S(2)}, u32[]{:S(2)}) collective-permute-start(bf16[32,7168]{1,0:T(8,128)(2,1)S(1)} %reshape.11.refs_5_), channel_id=1, source_target_pairs={{32,0},{112,16},{64,32},{16,48},{96,64},{48,80},{0,96},{80,112},{3... | collective-permute-start | bytes 1376264 | tf_op jit(solution)/shard_map/ppermute | solution.py:222
  24.0 9.9 %collective-permute-start = (bf16[32,7168]{1,0:T(8,128)(2,1)S(1)}, bf16[32,7168]{1,0:T(8,128)(2,1)S(1)}, u32[]{:S(2)}, u32[]{:S(2)}) collective-permute-start(bf16[32,7168]{1,0:T(8,128)(2,1)S(1)} %reshape.11.refs_5_), channel_id=1, source_target_pairs={{0,32},{16,112},{32,64},{48,16},{64,96},{80,48},{96,0},{112,80},{1... | collective-permute-start | bytes 1376264 | tf_op jit(solution)/shard_map/ppermute | solution.py:221
  24.0 0.7 copy-start.6
  24.6 13.3 %copy-start = (bf16[1,7168,256]{2,1,0:T(8,128)(2,1)S(1)}, bf16[1,7168,256]{2,1,0:T(8,128)(2,1)}, u32[]{:S(2)}) copy-start(bf16[1,7168,256]{2,1,0:T(8,128)(2,1)} %refs_2_.1) | copy-start | bytes 11010052
  24.7 13.3 %copy-start.1 = (bf16[1,7168,256]{2,1,0:T(8,128)(2,1)S(1)}, bf16[1,7168,256]{2,1,0:T(8,128)(2,1)}, u32[]{:S(2)}) copy-start(bf16[1,7168,256]{2,1,0:T(8,128)(2,1)} %refs_3_.1) | copy-start | bytes 11010052
  24.7 13.3 %copy-start.2 = (bf16[1,256,7168]{2,1,0:T(8,128)(2,1)S(1)}, bf16[1,256,7168]{2,1,0:T(8,128)(2,1)}, u32[]{:S(2)}) copy-start(bf16[1,256,7168]{2,1,0:T(8,128)(2,1)} %refs_4_.1) | copy-start | bytes 11010052
  33.8 2.5 %collective-permute-start.3 = (bf16[32,7168]{1,0:T(8,128)(2,1)S(1)}, bf16[32,7168]{1,0:T(8,128)(2,1)S(1)}, u32[]{:S(2)}, u32[]{:S(2)}) collective-permute-start(bf16[32,7168]{1,0:T(8,128)(2,1)S(1)} %reshape.11.refs_5_), channel_id=1, source_target_pairs={{0,16},{16,0},{1,17},{17,1},{2,18},{18,2},{3,19},{19,3},{4,20},{20... | collective-permute-start | bytes 1376264 | tf_op jit(solution)/shard_map/ppermute | solution.py:223
  33.9 9.8 %collective-permute-start.2 = (bf16[32,7168]{1,0:T(8,128)(2,1)S(1)}, bf16[32,7168]{1,0:T(8,128)(2,1)S(1)}, u32[]{:S(2)}, u32[]{:S(2)}) collective-permute-start(bf16[32,7168]{1,0:T(8,128)(2,1)S(1)} %collective-permute-done.refs_6_), channel_id=1, source_target_pairs={{0,32},{16,112},{32,64},{48,16},{64,96},{80,48},{96,0},{112,80},{1... | collective-permute-start | bytes 1376264 | tf_op jit(solution)/shard_map/ppermute | solution.py:227
  34.7 2.1 %collective-permute-start.7 = (bf16[16,7168]{1,0:T(8,128)(2,1)S(1)}, bf16[16,7168]{1,0:T(8,128)(2,1)S(1)}, u32[]{:S(2)}, u32[]{:S(2)}) collective-permute-start(bf16[16,7168]{1,0:T(8,128)(2,1)S(1)} %get-tuple-element.24), channel_id=1, source_target_pairs={{0,16},{16,0},{1,17},{17,1},{2,18},{18,2},{3,19},{19,3},{4,20},{20... | collective-permute-start | bytes 688136 | tf_op jit(solution)/shard_map/ppermute | solution.py:231
  35.8 1.5 %collective-permute-start.6 = (bf16[16,7168]{1,0:T(8,128)(2,1)S(1)}, bf16[16,7168]{1,0:T(8,128)(2,1)S(1)}, u32[]{:S(2)}, u32[]{:S(2)}) collective-permute-start(bf16[16,7168]{1,0:T(8,128)(2,1)S(1)} %get-tuple-element.25), channel_id=1, source_target_pairs={{0,16},{16,0},{1,17},{17,1},{2,18},{18,2},{3,19},{19,3},{4,20},{20... | collective-permute-start | bytes 688136 | tf_op jit(solution)/shard_map/ppermute | solution.py:231
  35.9 1.7 %collective-permute-start.5 = (bf16[16,7168]{1,0:T(8,128)(2,1)S(1)}, bf16[16,7168]{1,0:T(8,128)(2,1)S(1)}, u32[]{:S(2)}, u32[]{:S(2)}) collective-permute-start(bf16[16,7168]{1,0:T(8,128)(2,1)S(1)} %get-tuple-element.26), channel_id=1, source_target_pairs={{0,16},{16,0},{1,17},{17,1},{2,18},{18,2},{3,19},{19,3},{4,20},{20... | collective-permute-start | bytes 688136 | tf_op jit(solution)/shard_map/ppermute | solution.py:231
  36.3 1.6 %collective-permute-start.4 = (bf16[16,7168]{1,0:T(8,128)(2,1)S(1)}, bf16[16,7168]{1,0:T(8,128)(2,1)S(1)}, u32[]{:S(2)}, u32[]{:S(2)}) collective-permute-start(bf16[16,7168]{1,0:T(8,128)(2,1)S(1)} %get-tuple-element.27), channel_id=1, source_target_pairs={{0,16},{16,0},{1,17},{17,1},{2,18},{18,2},{3,19},{19,3},{4,20},{20... | collective-permute-start | bytes 688136 | tf_op jit(solution)/shard_map/ppermute | solution.py:231
  43.7 1.8 %collective-permute-start.11 = (bf16[32,7168]{1,0:T(8,128)(2,1)S(1)}, bf16[32,7168]{1,0:T(8,128)(2,1)S(1)}, u32[]{:S(2)}, u32[]{:S(2)}) collective-permute-start(bf16[32,7168]{1,0:T(8,128)(2,1)S(1)} %collective-permute-done.2.refs_1_), channel_id=1, source_target_pairs={{0,16},{16,0},{1,17},{17,1},{2,18},{18,2},{3,19},{19,3},{4,20},{20... | collective-permute-start | bytes 1376264 | tf_op jit(solution)/shard_map/ppermute | solution.py:236
  43.7 4.1 %collective-permute-start.8 = (bf16[32,7168]{1,0:T(8,128)(2,1)S(1)}, bf16[32,7168]{1,0:T(8,128)(2,1)S(1)}, u32[]{:S(2)}, u32[]{:S(2)}) collective-permute-start(bf16[32,7168]{1,0:T(8,128)(2,1)S(1)} %get-tuple-element.17), channel_id=1, source_target_pairs={{0,16},{16,0},{1,17},{17,1},{2,18},{18,2},{3,19},{19,3},{4,20},{20... | collective-permute-start | bytes 1376264 | tf_op jit(solution)/shard_map/ppermute | solution.py:234
  44.2 3.6 %collective-permute-start.9 = (bf16[32,7168]{1,0:T(8,128)(2,1)S(1)}, bf16[32,7168]{1,0:T(8,128)(2,1)S(1)}, u32[]{:S(2)}, u32[]{:S(2)}) collective-permute-start(bf16[32,7168]{1,0:T(8,128)(2,1)S(1)} %get-tuple-element.18), channel_id=1, source_target_pairs={{0,16},{16,0},{1,17},{17,1},{2,18},{18,2},{3,19},{19,3},{4,20},{20... | collective-permute-start | bytes 1376264 | tf_op jit(solution)/shard_map/ppermute | solution.py:234
  44.2 3.6 %collective-permute-start.10 = (bf16[32,7168]{1,0:T(8,128)(2,1)S(1)}, bf16[32,7168]{1,0:T(8,128)(2,1)S(1)}, u32[]{:S(2)}, u32[]{:S(2)}) collective-permute-start(bf16[32,7168]{1,0:T(8,128)(2,1)S(1)} %get-tuple-element.19), channel_id=1, source_target_pairs={{0,16},{16,0},{1,17},{17,1},{2,18},{18,2},{3,19},{19,3},{4,20},{20... | collective-permute-start | bytes 1376264 | tf_op jit(solution)/shard_map/ppermute | solution.py:234
  47.6 1.9 %collective-permute-start.12 = (bf16[32,7168]{1,0:T(8,128)(2,1)S(1)}, bf16[32,7168]{1,0:T(8,128)(2,1)S(1)}, u32[]{:S(2)}, u32[]{:S(2)}) collective-permute-start(bf16[32,7168]{1,0:T(8,128)(2,1)S(1)} %get-tuple-element.22), channel_id=1, source_target_pairs={{0,16},{16,0},{1,17},{17,1},{2,18},{18,2},{3,19},{19,3},{4,20},{20... | collective-permute-start | bytes 1376264 | tf_op jit(solution)/shard_map/ppermute | solution.py:237
  49.5 32.8 %copy-start.4 = (s32[6,2]{0,1:T(2,128)S(1)}, s32[6,2]{0,1:T(2,128)}, u32[]{:S(2)}) copy-start(s32[6,2]{0,1:T(2,128)} %param.10) | copy-start | bytes 148
  49.5 32.8 %copy-start.5 = (f32[6,2]{0,1:T(2,128)S(1)}, f32[6,2]{0,1:T(2,128)}, u32[]{:S(2)}) copy-start(f32[6,2]{0,1:T(2,128)} %param.11) | copy-start | bytes 148
